TPU v7x, 32 devices: a whole 2x2x4 slice. The times are simulated.
32 devices in a mesh: dp: 8 (over z, core), fsdp: 4 (over y, x).
Axes of the slice: x: 2, y: 2, z: 4, core: 2. Of those that a mesh axis runs over, the one named last changes fastest.
Arguments:
- tokens: bfloat16 [8192, 1024], P(('dp', 'fsdp')), may hold values from -6 to 6
- memory: bfloat16 [4096, 1024], P(('dp', 'fsdp')), may hold values from -6 to 6
- target_segments: int32 [32, 256], P(('dp', 'fsdp')), may hold values from 0 to 3, never falling along the last dimension, each value on 1 to 192 neighbouring positions
- source_segments: int32 [32, 128], P(('dp', 'fsdp')), may hold values from 0 to 3, never falling along the last dimension, each value on 1 to 96 neighbouring positions
- self_query: bfloat16 [1024, 1024], P(('dp', 'fsdp')), may hold values from -0.1875 to 0.1875
- self_key: bfloat16 [1024, 1024], P(('dp', 'fsdp')), may hold values from -0.1875 to 0.1875
- self_value: bfloat16 [1024, 1024], P(('dp', 'fsdp')), may hold values from -0.1875 to 0.1875
- self_output: bfloat16 [1024, 1024], P(('dp', 'fsdp')), may hold values from -2 to 2
- cross_query: bfloat16 [1024, 1024], P(('dp', 'fsdp')), may hold values from -0.1875 to 0.1875
- cross_key: bfloat16 [1024, 1024], P(('dp', 'fsdp')), may hold values from -0.1875 to 0.1875
- cross_value: bfloat16 [1024, 1024], P(('dp', 'fsdp')), may hold values from -0.1875 to 0.1875
- cross_output: bfloat16 [1024, 1024], P(('dp', 'fsdp')), may hold values from -2 to 2
- expand_weight: bfloat16 [1024, 4096], P(('dp', 'fsdp')), may hold values from -0.1875 to 0.1875
- reduce_weight: bfloat16 [4096, 1024], P(('dp', 'fsdp')), may hold values from -0.75 to 0.75
- self_gain: bfloat16 [1024], P(('dp', 'fsdp')), may hold values from 0.099609375 to 1.8984375
- self_shift: bfloat16 [1024], P(('dp', 'fsdp')), may hold values from -3 to 3
- cross_gain: bfloat16 [1024], P(('dp', 'fsdp')), may hold values from 0.099609375 to 1.8984375
- cross_shift: bfloat16 [1024], P(('dp', 'fsdp')), may hold values from -3 to 3
- final_gain: bfloat16 [1024], P(('dp', 'fsdp')), may hold values from 0.099609375 to 1.8984375
- final_shift: bfloat16 [1024], P(('dp', 'fsdp')), may hold values from -3 to 3
- output_grad: bfloat16 [8192, 1024], P(('dp', 'fsdp')), may hold values from -6 to 6
Outputs:
- output: bfloat16 [8192, 1024], P(('dp', 'fsdp'))
- tokens_grad: float32 [8192, 1024], P(('dp', 'fsdp'))
- memory_grad: float32 [4096, 1024], P(('dp', 'fsdp'))
- self_query_grad: float32 [1024, 1024], P(('dp', 'fsdp'))
- self_key_grad: float32 [1024, 1024], P(('dp', 'fsdp'))
- self_value_grad: float32 [1024, 1024], P(('dp', 'fsdp'))
- self_output_grad: float32 [1024, 1024], P(('dp', 'fsdp'))
- cross_query_grad: float32 [1024, 1024], P(('dp', 'fsdp'))
- cross_key_grad: float32 [1024, 1024], P(('dp', 'fsdp'))
- cross_value_grad: float32 [1024, 1024], P(('dp', 'fsdp'))
- cross_output_grad: float32 [1024, 1024], P(('dp', 'fsdp'))
- expand_weight_grad: float32 [1024, 4096], P(('dp', 'fsdp'))
- reduce_weight_grad: float32 [4096, 1024], P(('dp', 'fsdp'))
- self_gain_grad: float32 [1024], P(('dp', 'fsdp'))
- self_shift_grad: float32 [1024], P(('dp', 'fsdp'))
- cross_gain_grad: float32 [1024], P(('dp', 'fsdp'))
- cross_shift_grad: float32 [1024], P(('dp', 'fsdp'))
- final_gain_grad: float32 [1024], P(('dp', 'fsdp'))
- final_shift_grad: float32 [1024], P(('dp', 'fsdp'))
Inputs may be any that keep to these rules, and one draw needn't show every extreme that they name: `target_segments`: each row numbers its positions by sentence, 0 to 3 in order and never falling, every sentence with 1 to 192 positions. `source_segments`: each row numbers its positions by sentence, 0 to 3 in order and never falling, every sentence with 1 to 96 positions; source sentence j of a pack belongs to target sentence j of the same pack.
All inputs are finite; a program needn't handle non-finite values.
Results may differ from a plain program's by a relative error of at most 0.02.
The roundings to bfloat16 on the way count: a program that leaves them out, or rounds other values in their place, can miss the bound.
Values may be sent and summed in bfloat16 or wider, within the bound.
No kernel may reach another device: no remote copies, remote signals or barrier semaphores. Data moves between devices by JAX's collectives and lax.ppermute only.
A program may use at most 320 MiB of HBM per device.

v0:
```python
import jax
import jax.numpy as jnp
from jax import lax
from jax.sharding import PartitionSpec as P

HEADS = 16
HEAD_DIM = 64


RESIDUAL_SCALE = 300.0**0.25
EPSILON = 1e-05
NEGATIVE = -1e30


def fetch(attention_rows, expand_rows, reduce_rows, norm_rows):
    gathered = (
        lax.all_gather(attention_rows, ("dp", "fsdp"), axis=1, tiled=True),
        lax.all_gather(expand_rows, ("dp", "fsdp"), axis=0, tiled=True),
        lax.all_gather(reduce_rows, ("dp", "fsdp"), axis=0, tiled=True),
        lax.all_gather(norm_rows, ("dp", "fsdp"), axis=1, tiled=True),
    )
    return gathered


def settle(attention_terms, expand_terms, reduce_terms, norm_terms):
    owned = (
        lax.psum_scatter(attention_terms, ("dp", "fsdp"), scatter_dimension=1, tiled=True),
        lax.psum_scatter(expand_terms, ("dp", "fsdp"), scatter_dimension=0, tiled=True),
        lax.psum_scatter(reduce_terms, ("dp", "fsdp"), scatter_dimension=0, tiled=True),
        lax.psum_scatter(norm_terms, ("dp", "fsdp"), scatter_dimension=1, tiled=True),
    )
    return owned


def matmul(left, right):
    return jnp.dot(left, right, preferred_element_type=jnp.float32)


def across(left, right):
    return jnp.einsum("ti,tj->ij", left, right, preferred_element_type=jnp.float32)


def against(left, right):
    return jnp.einsum("ti,ji->tj", left, right, preferred_element_type=jnp.float32)


def gelu_tanh(values):
    return jax.nn.gelu(values, approximate=True)


def normalize(summed, gain, shift):
    center = jnp.mean(summed, axis=-1, keepdims=True)
    centred = summed - center
    inverse = lax.rsqrt(jnp.mean(centred * centred, axis=-1, keepdims=True) + EPSILON)
    scaled = centred * inverse
    return (scaled * gain + shift, scaled, inverse)


def normalize_back(incoming, scaled, inverse, gain):
    spread = incoming * gain
    d_summed = inverse * (
        spread
        - jnp.mean(spread, axis=-1, keepdims=True)
        - scaled * jnp.mean(spread * scaled, axis=-1, keepdims=True)
    )
    return (d_summed, jnp.sum(incoming * scaled, axis=0), jnp.sum(incoming, axis=0))


def split_heads(matrix):
    return matrix.reshape(matrix.shape[0], HEADS, HEAD_DIM)


def scores_of(query_rows, key_rows, allowed):
    raw = jnp.einsum(
        "qhd,khd->hqk",
        split_heads(query_rows),
        split_heads(key_rows),
        preferred_element_type=jnp.float32,
    ) * HEAD_DIM ** (-0.5)
    return jnp.where(allowed[None], raw, NEGATIVE)


def attend_forward(query_rows, key_rows, value_rows, allowed):
    scores = scores_of(query_rows, key_rows, allowed)
    highest = jnp.max(scores, axis=-1, keepdims=True)
    weights = jnp.exp(scores - highest)
    totals = jnp.sum(weights, axis=-1, keepdims=True)
    chances = (weights / totals).astype(jnp.bfloat16)
    context = jnp.einsum(
        "hqk,khd->qhd", chances, split_heads(value_rows), preferred_element_type=jnp.float32
    )
    return (
        context.reshape(query_rows.shape[0], HEADS * HEAD_DIM).astype(jnp.bfloat16),
        highest + jnp.log(totals),
    )


def attend_back(query_rows, key_rows, value_rows, allowed, logsum, d_context):
    query_heads = split_heads(query_rows)
    key_heads = split_heads(key_rows)
    d_heads = split_heads(d_context)
    chances = jnp.exp(scores_of(query_rows, key_rows, allowed) - logsum)
    d_chances = jnp.einsum(
        "qhd,khd->hqk", d_heads, split_heads(value_rows), preferred_element_type=jnp.float32
    )
    d_value = jnp.einsum(
        "hqk,qhd->khd", chances.astype(jnp.bfloat16), d_heads, preferred_element_type=jnp.float32
    )
    centre = jnp.sum(d_chances * chances, axis=-1, keepdims=True)
    d_scores = (chances * (d_chances - centre)).astype(jnp.bfloat16)
    d_query = jnp.einsum(
        "hqk,khd->qhd", d_scores, key_heads, preferred_element_type=jnp.float32
    ) * HEAD_DIM ** (-0.5)
    d_key = jnp.einsum(
        "hqk,qhd->khd", d_scores, query_heads, preferred_element_type=jnp.float32
    ) * HEAD_DIM ** (-0.5)
    query_count = query_rows.shape[0]
    key_count = key_rows.shape[0]
    return (
        d_query.reshape(query_count, HEADS * HEAD_DIM).astype(jnp.bfloat16),
        d_key.reshape(key_count, HEADS * HEAD_DIM).astype(jnp.bfloat16),
        d_value.reshape(key_count, HEADS * HEAD_DIM).astype(jnp.bfloat16),
    )


def per_device(
    tokens,
    memory,
    target_segments,
    source_segments,
    self_query,
    self_key,
    self_value,
    self_output,
    cross_query,
    cross_key,
    cross_value,
    cross_output,
    expand_weight,
    reduce_weight,
    self_gain,
    self_shift,
    cross_gain,
    cross_shift,
    final_gain,
    final_shift,
    output_grad,
):
    attention_rows = jnp.stack(
        [
            self_query,
            self_key,
            self_value,
            self_output,
            cross_query,
            cross_key,
            cross_value,
            cross_output,
        ]
    )
    norm_rows = jnp.stack([self_gain, self_shift, cross_gain, cross_shift, final_gain, final_shift])
    matrices, expand_full, reduce_full, norm_full = fetch(
        attention_rows, expand_weight, reduce_weight, norm_rows
    )
    gains = norm_full.astype(jnp.float32)
    target_ids = target_segments[0]
    source_ids = source_segments[0]
    positions = lax.iota(jnp.int32, tokens.shape[0])
    causal = (target_ids[:, None] == target_ids[None, :]) & (
        positions[None, :] <= positions[:, None]
    )
    crossing = target_ids[:, None] == source_ids[None, :]
    query_one = matmul(tokens, matrices[0]).astype(jnp.bfloat16)
    key_one = matmul(tokens, matrices[1]).astype(jnp.bfloat16)
    value_one = matmul(tokens, matrices[2]).astype(jnp.bfloat16)
    context_one, logsum_one = attend_forward(query_one, key_one, value_one, causal)
    branch_one = matmul(context_one, matrices[3])
    first, first_scaled, first_inverse = normalize(
        RESIDUAL_SCALE * tokens.astype(jnp.float32) + branch_one, gains[0], gains[1]
    )
    first_low = first.astype(jnp.bfloat16)
    query_two = matmul(first_low, matrices[4]).astype(jnp.bfloat16)
    key_two = matmul(memory, matrices[5]).astype(jnp.bfloat16)
    value_two = matmul(memory, matrices[6]).astype(jnp.bfloat16)
    context_two, logsum_two = attend_forward(query_two, key_two, value_two, crossing)
    branch_two = matmul(context_two, matrices[7])
    second, second_scaled, second_inverse = normalize(
        RESIDUAL_SCALE * first + branch_two, gains[2], gains[3]
    )
    second_low = second.astype(jnp.bfloat16)
    inner = matmul(second_low, expand_full)
    active = gelu_tanh(inner).astype(jnp.bfloat16)
    branch_three = matmul(active, reduce_full)
    final, final_scaled, final_inverse = normalize(
        RESIDUAL_SCALE * second + branch_three, gains[4], gains[5]
    )
    output = final.astype(jnp.bfloat16)
    matrices, expand_full, reduce_full, norm_full = fetch(
        attention_rows, expand_weight, reduce_weight, norm_rows
    )
    gains = norm_full.astype(jnp.float32)
    d_sum_three, final_gain_term, final_shift_term = normalize_back(
        output_grad.astype(jnp.float32), final_scaled, final_inverse, gains[4]
    )
    d_branch_three = d_sum_three.astype(jnp.bfloat16)
    reduce_term = across(active, d_branch_three)
    d_active = against(d_branch_three, reduce_full)
    d_inner = jax.vjp(gelu_tanh, inner)[1](d_active)[0].astype(jnp.bfloat16)
    expand_term = across(second_low, d_inner)
    d_second = RESIDUAL_SCALE * d_sum_three + against(d_inner, expand_full)
    d_sum_two, cross_gain_term, cross_shift_term = normalize_back(
        d_second, second_scaled, second_inverse, gains[2]
    )
    d_branch_two = d_sum_two.astype(jnp.bfloat16)
    cross_output_term = across(context_two, d_branch_two)
    d_context_two = against(d_branch_two, matrices[7]).astype(jnp.bfloat16)
    d_query_two, d_key_two, d_value_two = attend_back(
        query_two, key_two, value_two, crossing, logsum_two, d_context_two
    )
    cross_query_term = across(first_low, d_query_two)
    cross_key_term = across(memory, d_key_two)
    cross_value_term = across(memory, d_value_two)
    memory_grad = against(d_key_two, matrices[5]) + against(d_value_two, matrices[6])
    d_first = RESIDUAL_SCALE * d_sum_two + against(d_query_two, matrices[4])
    d_sum_one, self_gain_term, self_shift_term = normalize_back(
        d_first, first_scaled, first_inverse, gains[0]
    )
    d_branch_one = d_sum_one.astype(jnp.bfloat16)
    self_output_term = across(context_one, d_branch_one)
    d_context_one = against(d_branch_one, matrices[3]).astype(jnp.bfloat16)
    d_query_one, d_key_one, d_value_one = attend_back(
        query_one, key_one, value_one, causal, logsum_one, d_context_one
    )
    self_query_term = across(tokens, d_query_one)
    self_key_term = across(tokens, d_key_one)
    self_value_term = across(tokens, d_value_one)
    tokens_grad = (
        RESIDUAL_SCALE * d_sum_one
        + against(d_query_one, matrices[0])
        + against(d_key_one, matrices[1])
        + against(d_value_one, matrices[2])
    )
    attention_terms = jnp.stack(
        [
            self_query_term,
            self_key_term,
            self_value_term,
            self_output_term,
            cross_query_term,
            cross_key_term,
            cross_value_term,
            cross_output_term,
        ]
    )
    norm_terms = jnp.stack(
        [
            self_gain_term,
            self_shift_term,
            cross_gain_term,
            cross_shift_term,
            final_gain_term,
            final_shift_term,
        ]
    )
    attention_owned, expand_owned, reduce_owned, norm_owned = settle(
        attention_terms, expand_term, reduce_term, norm_terms
    )
    return (
        output,
        tokens_grad,
        memory_grad,
        attention_owned[0],
        attention_owned[1],
        attention_owned[2],
        attention_owned[3],
        attention_owned[4],
        attention_owned[5],
        attention_owned[6],
        attention_owned[7],
        expand_owned,
        reduce_owned,
        norm_owned[0],
        norm_owned[1],
        norm_owned[2],
        norm_owned[3],
        norm_owned[4],
        norm_owned[5],
    )


def solution(mesh):
    return jax.shard_map(
        per_device,
        mesh=mesh,
        in_specs=(
            P(("dp", "fsdp"), None),
            P(("dp", "fsdp"), None),
            P(("dp", "fsdp"), None),
            P(("dp", "fsdp"), None),
            P(("dp", "fsdp"), None),
            P(("dp", "fsdp"), None),
            P(("dp", "fsdp"), None),
            P(("dp", "fsdp"), None),
            P(("dp", "fsdp"), None),
            P(("dp", "fsdp"), None),
            P(("dp", "fsdp"), None),
            P(("dp", "fsdp"), None),
            P(("dp", "fsdp"), None),
            P(("dp", "fsdp"), None),
            P(("dp", "fsdp")),
            P(("dp", "fsdp")),
            P(("dp", "fsdp")),
            P(("dp", "fsdp")),
            P(("dp", "fsdp")),
            P(("dp", "fsdp")),
            P(("dp", "fsdp"), None),
        ),
        out_specs=(
            P(("dp", "fsdp"), None),
            P(("dp", "fsdp"), None),
            P(("dp", "fsdp"), None),
            P(("dp", "fsdp"), None),
            P(("dp", "fsdp"), None),
            P(("dp", "fsdp"), None),
            P(("dp", "fsdp"), None),
            P(("dp", "fsdp"), None),
            P(("dp", "fsdp"), None),
            P(("dp", "fsdp"), None),
            P(("dp", "fsdp"), None),
            P(("dp", "fsdp"), None),
            P(("dp", "fsdp"), None),
            P(("dp", "fsdp")),
            P(("dp", "fsdp")),
            P(("dp", "fsdp")),
            P(("dp", "fsdp")),
            P(("dp", "fsdp")),
            P(("dp", "fsdp")),
        ),
        check_vma=False,
    )
```

profile of v0, /device:TPU:0, one launch (start us, length us, event | category | flops | bytes accessed | tf_op | source)
XLA Modules:
  0.0 1913.6 jit_solution(2729841898250139384)
XLA Ops:
  17.2 71.5 %all-gather = bf16[32,32,6]{1,2,0:T(8,128)(2,1)S(1)} all-gather(bf16[1,32,6]{1,2,0:T(8,128)(2,1)S(1)} %bitcast.330), channel_id=1, replica_groups=mesh['dp'=8,'fsdp'=4] {'dp','fsdp'}, dimensions={0}, use_global_device_ids=true | all-gather | bytes 12672 | tf_op jit(solution)/shard_map/all_gather | solution.py:20
  90.5 42.1 %all-gather.5.cloned.1.call-done = bf16[8,1024,1024]{2,1,0:T(8,128)(2,1)} async-done(((bf16[8,32,1024]{2,1,0:T(8,128)(2,1)}), bf16[8,1024,1024]{2,1,0:T(8,128)(2,1)}) %all-gather.5.cloned.1.call-update) | async-done | bytes 16777232 | tf_op jit(solution)/shard_map/all_gather | solution.py:17
  139.1 3.3 fusion.49
  161.5 49.4 %all-gather.7.cloned.1.call-done = bf16[1024,4096]{1,0:T(8,128)(2,1)} async-done(((bf16[32,4096]{1,0:T(8,128)(2,1)}), bf16[1024,4096]{1,0:T(8,128)(2,1)}) %all-gather.7.cloned.1.call-update) | async-done | bytes 8388624 | tf_op jit(solution)/shard_map/all_gather | solution.py:18
  210.9 8.1 fusion.78
  219.0 71.0 %all-gather.9.cloned.1.call-done = bf16[4096,1024]{1,0:T(8,128)(2,1)} async-done(((bf16[128,1024]{1,0:T(8,128)(2,1)}), bf16[4096,1024]{1,0:T(8,128)(2,1)}) %all-gather.9.cloned.1.call-update) | async-done | bytes 8388624 | tf_op jit(solution)/shard_map/all_gather | solution.py:19
  289.9 8.1 fusion.91
  299.7 8.2 fusion.6
  307.9 7.1 multiply_reduce_fusion.2
  316.4 3.2 fusion.44
  328.0 3.0 multiply_reduce_fusion.3
  331.4 3.2 fusion.46
  335.8 3.9 fusion.40
  356.0 2.9 bitcast_dynamic-update-slice_fusion.6
  366.9 33.0 %copy.119 = f32[8,1024,1024]{2,0,1:T(8,128)} copy(f32[8,1024,1024]{1,2,0:T(8,128)} %bitcast_dynamic-update-slice_fusion.5) | data formatting | bytes 67108864 | tf_op jit(solution)/shard_map/stack | solution.py:243
  401.1 11.1 fusion.69
  413.5 9.8 fusion.76
  425.8 3.2 fusion.53
  433.8 3.4 fusion.38
  437.2 40.6 %reduce-scatter.13.cloned.1.call-done = f32[32,6]{1,0:T(8,128)} async-done(((f32[1024,6]{1,0:T(8,128)}), f32[32,6]{1,0:T(8,128)}) %reduce-scatter.13.cloned.1.call-update) | async-done | bytes 784
  482.3 701.6 %reduce-scatter.7.cloned.1.call-done = f32[8,32,1024]{2,0,1:T(8,128)} async-done(((f32[8,1024,1024]{2,0,1:T(8,128)}), f32[8,32,1024]{2,0,1:T(8,128)}) %reduce-scatter.7.cloned.1.call-update) | async-done | bytes 1048592 | tf_op jit(solution)/shard_map/reduce_scatter | solution.py:27
  1183.9 5.4 fusion.84
  1194.7 349.8 %reduce-scatter.11.cloned.1.call-done = f32[128,1024]{1,0:T(8,128)} async-done(((f32[4096,1024]{1,0:T(8,128)}), f32[128,1024]{1,0:T(8,128)}) %reduce-scatter.11.cloned.1.call-update) | async-done | bytes 524304 | tf_op jit(solution)/shard_map/reduce_scatter | solution.py:29
  1544.5 362.1 %reduce-scatter.9.cloned.1.call-done = f32[32,4096]{1,0:T(8,128)} async-done(((f32[1024,4096]{1,0:T(8,128)}), f32[32,4096]{1,0:T(8,128)}) %reduce-scatter.9.cloned.1.call-update) | async-done | bytes 524304 | tf_op jit(solution)/shard_map/reduce_scatter | solution.py:28
  (177 shorter events, 93.8 us)
Async XLA Ops:
  7.2 142.3 %copy-start = (bf16[128,1024]{1,0:T(8,128)(2,1)S(1)}, bf16[128,1024]{1,0:T(8,128)(2,1)}, u32[]{:S(2)}) copy-start(bf16[128,1024]{1,0:T(8,128)(2,1)} %param.22) | copy-start | bytes 786436
  7.2 125.4 %all-gather.5.cloned.1.call-start = ((), (), s32[]{:S(2)}) async-start(), calls=%async_computation.4 | async-start | bytes 17301504 | tf_op jit(solution)/shard_map/all_gather | solution.py:17
  14.9 196.0 %all-gather.7.cloned.1.call-start = ((), (), s32[]{:S(2)}) async-start(), calls=%async_computation.5 | async-start | bytes 8650752 | tf_op jit(solution)/shard_map/all_gather | solution.py:18
  15.6 274.3 %all-gather.9.cloned.1.call-start = ((), (), s32[]{:S(2)}) async-start(), calls=%async_computation.6 | async-start | bytes 8650752 | tf_op jit(solution)/shard_map/all_gather | solution.py:19
  16.3 461.4 %reduce-scatter.13.cloned.1.call-start = ((), (), s32[]{:S(2)}) async-start(), calls=%async_computation.10 | async-start | bytes 540672
  16.4 118.6 %copy-start.8 = (bf16[256,1024]{1,0:T(8,128)(2,1)S(1)}, bf16[256,1024]{1,0:T(8,128)(2,1)}, u32[]{:S(2)}) copy-start(bf16[256,1024]{1,0:T(8,128)(2,1)} %param.21) | copy-start | bytes 1572868
  138.5 3.9 copy-start.1
  157.5 3.9 copy-start.30
  289.9 8.4 copy-start.22
  289.9 9.8 copy-start.12
  298.0 9.9 copy-start.6
  299.7 8.2 copy-start.4
  307.9 7.1 copy-start.29
  331.4 8.4 copy-start.37
  335.8 4.0 copy-start.2
  341.9 3.4 copy-start.9
  345.1 838.9 %reduce-scatter.7.cloned.1.call-start = ((), (), s32[]{:S(2)}) async-start(), calls=%async_computation.7 | async-start | bytes 34603008 | tf_op jit(solution)/shard_map/reduce_scatter | solution.py:27
  356.0 5.5 copy-start.34
  358.9 5.3 copy-start.16
  358.9 5.3 copy-start.31
  399.9 1144.6 %reduce-scatter.11.cloned.1.call-start = ((), (), s32[]{:S(2)}) async-start(), calls=%async_computation.9 | async-start | bytes 17301504 | tf_op jit(solution)/shard_map/reduce_scatter | solution.py:29
  412.3 1494.3 %reduce-scatter.9.cloned.1.call-start = ((), (), s32[]{:S(2)}) async-start(), calls=%async_computation.8 | async-start | bytes 17301504 | tf_op jit(solution)/shard_map/reduce_scatter | solution.py:28
  423.3 5.7 copy-start.20
  429.0 4.8 copy-start.11
  (22 other events, 41.2 us)
Sparse Core Ops, SparseCore 0:
  15.0 117.5 all-gather.4
  135.4 75.3 all-gather.6
  213.7 76.1 all-gather.8
  345.2 132.5 reduce-scatter.12
  480.0 703.8 reduce-scatter.6
  1186.7 357.7 reduce-scatter.10
  1547.5 359.0 reduce-scatter.8
where the time goes:
time: 1920 us; the launch traced here: 1910 us
  waiting for transfers between devices  1620 us (84%)
  matrix products  134 us (7%)
  blocking collectives  71.5 us (4%)
  local copies, waits for them, and re-layouts  67.2 us (4%)
    reduce_scatter x1, waiting for transfers between devices, settle(): lax.psum_scatter(attention_terms, ('dp', 'fsdp'), scatter_dimension=1, ti...  702 us
    reduce_scatter x1, waiting for transfers between devices, settle(): lax.psum_scatter(expand_terms, ('dp', 'fsdp'), scatter_dimension=0, tiled...  362 us
    reduce_scatter x1, waiting for transfers between devices, settle(): lax.psum_scatter(reduce_terms, ('dp', 'fsdp'), scatter_dimension=0, tiled...  350 us
    all_gather x1, blocking collectives, fetch(): lax.all_gather(norm_rows, ('dp', 'fsdp'), axis=1, tiled=True)  71.5 us
    all_gather x1, waiting for transfers between devices, fetch(): lax.all_gather(reduce_rows, ('dp', 'fsdp'), axis=0, tiled=True)  71 us
    all_gather x1, waiting for transfers between devices, fetch(): lax.all_gather(expand_rows, ('dp', 'fsdp'), axis=0, tiled=True)  49.4 us
    dot_general x10, matrix products, across(): jnp.einsum('ti,tj->ij', left, right, preferred_element_type=jnp.float32)  42.5 us
    all_gather x1, waiting for transfers between devices, fetch(): lax.all_gather(attention_rows, ('dp', 'fsdp'), axis=1, tiled=True)  42.1 us
  transfers between devices with their start and end apart: 7, of which 7 were waited for; matrix products, arithmetic and copies ran while one was open for 7% of the time, Pallas kernels for 0%

commit v1 on v0

--- a/solution.py
+++ b/solution.py
@@ -1,6 +1,10 @@
+import functools
+
 import jax
 import jax.numpy as jnp
 from jax import lax
+from jax.experimental import pallas as pl
+from jax.experimental.pallas import tpu as pltpu
 from jax.sharding import PartitionSpec as P
 
 HEADS = 16
@@ -10,26 +14,158 @@
 RESIDUAL_SCALE = 300.0**0.25
 EPSILON = 1e-05
 NEGATIVE = -1e30
-
-
-def fetch(attention_rows, expand_rows, reduce_rows, norm_rows):
-    gathered = (
-        lax.all_gather(attention_rows, ("dp", "fsdp"), axis=1, tiled=True),
-        lax.all_gather(expand_rows, ("dp", "fsdp"), axis=0, tiled=True),
-        lax.all_gather(reduce_rows, ("dp", "fsdp"), axis=0, tiled=True),
-        lax.all_gather(norm_rows, ("dp", "fsdp"), axis=1, tiled=True),
-    )
-    return gathered
-
-
-def settle(attention_terms, expand_terms, reduce_terms, norm_terms):
-    owned = (
-        lax.psum_scatter(attention_terms, ("dp", "fsdp"), scatter_dimension=1, tiled=True),
-        lax.psum_scatter(expand_terms, ("dp", "fsdp"), scatter_dimension=0, tiled=True),
-        lax.psum_scatter(reduce_terms, ("dp", "fsdp"), scatter_dimension=0, tiled=True),
-        lax.psum_scatter(norm_terms, ("dp", "fsdp"), scatter_dimension=1, tiled=True),
-    )
-    return owned
+ALL = ("dp", "fsdp")
+
+
+class Grid:
+    def __init__(self, mesh):
+        self.depth = mesh.shape["dp"] // 2
+        self.plane = mesh.shape["fsdp"]
+        self.count = mesh.size
+        self.fast = self.plane == 4 and mesh.shape["dp"] % 2 == 0
+
+    def place(self):
+        index = lax.axis_index(ALL)
+        return jnp.stack([index // 8, index // 4 % 2, index // 2 % 2, index % 2]).astype(jnp.int32)
+
+    def move(self, value, dz=0, dc=0, dy=0, dx=0):
+        pairs = []
+        for index in range(self.count):
+            z, c, y, x = index // 8, index // 4 % 2, index // 2 % 2, index % 2
+            source = (((z + dz) % self.depth * 2 + (c ^ dc)) * 2 + (y ^ dy)) * 2 + (x ^ dx)
+            pairs.append((source, index))
+        return lax.ppermute(value, ALL, pairs)
+
+
+def collect(grid, shard):
+    half = grid.depth // 2
+    own = jnp.stack([shard] + [grid.move(shard, dz=k) for k in range(1, grid.depth)])
+    over_x = grid.move(own, dx=1)
+    over_y = grid.move(own, dy=1)
+    low = grid.move(over_x[:half], dy=1)
+    high = grid.move(over_y[half:], dx=1)
+    near = [((0, 0, 0), 0, own), ((0, 0, 1), 0, over_x), ((0, 1, 0), 0, over_y)]
+    near += [((0, 1, 1), 0, low), ((0, 1, 1), half, high)]
+    far = [((1, dy, dx), first, grid.move(piece, dc=1)) for (_, dy, dx), first, piece in near]
+    return near + far
+
+
+def assemble_kernel(spots, depth, rows, place, *refs):
+    pieces, whole, sems = refs[:-2], refs[-2], refs[-1]
+    z, c, y, x = place[0], place[1], place[2], place[3]
+    copies = []
+    for (offsets, first, count), piece in zip(spots, pieces):
+        dc, dy, dx = offsets
+        for k in range(count):
+            there = lax.rem(z + (first + k), depth)
+            owner = ((there * 2 + (c ^ dc)) * 2 + (y ^ dy)) * 2 + (x ^ dx)
+            spot = pl.ds(pl.multiple_of(owner * rows, rows), rows)
+            target = whole.at[:, spot, :] if len(whole.shape) == 3 else whole.at[spot, :]
+            copies.append(pltpu.make_async_copy(piece.at[k], target, sems.at[len(copies)]))
+    for copy in copies:
+        copy.start()
+    for copy in copies:
+        copy.wait()
+
+
+def assemble(grid, place, pieces):
+    shape = pieces[0][2].shape[1:]
+    rows = shape[-2]
+    spots = tuple((offsets, first, piece.shape[0]) for offsets, first, piece in pieces)
+    whole = shape[:-2] + (rows * grid.count, shape[-1])
+    return pl.pallas_call(
+        functools.partial(assemble_kernel, spots, grid.depth, rows),
+        out_shape=jax.ShapeDtypeStruct(whole, jnp.bfloat16),
+        in_specs=[pl.BlockSpec(memory_space=pltpu.SMEM)]
+        + [pl.BlockSpec(memory_space=pl.ANY)] * len(pieces),
+        out_specs=pl.BlockSpec(memory_space=pl.ANY),
+        scratch_shapes=[pltpu.SemaphoreType.DMA((grid.count,))],
+        cost_estimate=pl.CostEstimate(
+            flops=0, bytes_accessed=4 * grid.count * pieces[0][2][0].size, transcendentals=0
+        ),
+        name="assemble",
+    )(place, *[piece for _, _, piece in pieces])
+
+
+def terms_kernel(depth, rows, place, left, left_far, right, right_far, own, over_x, over_y, low, high, turned):
+    z, c, y, x = place[0], place[1], place[2], place[3]
+    tokens = left.shape[0]
+
+    @pl.when(pl.program_id(0) == 0)
+    def _():
+        for k in range(depth):
+            there = lax.rem(z + k, depth)
+            columns = pl.ds(pl.multiple_of((there * 2 + c) * (4 * rows), 4 * rows), 4 * rows)
+            for side, source in enumerate((left, left_far)):
+                block = source[:, columns].T
+                for dy in range(2):
+                    for dx in range(2):
+                        near = (dy ^ y) * 2 + (dx ^ x)
+                        spot = dy * 2 + dx
+                        turned[near, k * rows : (k + 1) * rows, side * tokens : (side + 1) * tokens] = block[
+                            spot * rows : (spot + 1) * rows
+                        ]
+
+    half = depth // 2
+    for spot in range(4):
+        part = turned[spot]
+        total = jnp.dot(part[:, :tokens], right[...], preferred_element_type=jnp.float32)
+        total += jnp.dot(part[:, tokens:], right_far[...], preferred_element_type=jnp.float32)
+        total = total.astype(jnp.bfloat16).reshape(depth, rows, -1)
+        if spot == 0:
+            own[...] = total
+        elif spot == 1:
+            over_x[...] = total
+        elif spot == 2:
+            over_y[...] = total
+        else:
+            low[...] = total[:half]
+            high[...] = total[half:]
+
+
+def terms(grid, place, left, left_far, right, right_far, tile):
+    tokens, features = left.shape
+    width = right.shape[1]
+    rows = features // grid.count
+    depth = grid.depth
+    counts = (depth, depth, depth, depth // 2, depth // 2)
+    return pl.pallas_call(
+        functools.partial(terms_kernel, depth, rows),
+        grid=(width // tile,),
+        out_shape=[jax.ShapeDtypeStruct((n, rows, width), jnp.bfloat16) for n in counts],
+        in_specs=[pl.BlockSpec(memory_space=pltpu.SMEM)]
+        + [pl.BlockSpec((tokens, features), lambda j: (0, 0))] * 2
+        + [pl.BlockSpec((tokens, tile), lambda j: (0, j))] * 2,
+        out_specs=[pl.BlockSpec((n, rows, tile), lambda j: (0, 0, j)) for n in counts],
+        scratch_shapes=[pltpu.VMEM((4, depth * rows, 2 * tokens), jnp.bfloat16)],
+        compiler_params=pltpu.CompilerParams(vmem_limit_bytes=40 * 2**20),
+        cost_estimate=pl.CostEstimate(
+            flops=2 * tokens * features * width,
+            bytes_accessed=4 * tokens * (features + width) + features * width,
+            transcendentals=0,
+        ),
+        name="terms",
+    )(place, left, left_far, right, right_far)
+
+
+def settle(grid, pieces):
+    own, over_x, over_y, low, high = pieces
+    half = grid.depth // 2
+    got_low = grid.move(low, dy=1)
+    got_high = grid.move(high, dx=1)
+    wide = jnp.float32
+    over_x = over_x.at[:half].add(got_low)
+    over_y = over_y.at[half:].add(got_high)
+    got_x = grid.move(over_x, dx=1)
+    got_y = grid.move(over_y, dy=1)
+    column = [
+        (own[k].astype(wide) + got_x[k].astype(wide) + got_y[k].astype(wide)).astype(jnp.bfloat16)
+        for k in range(grid.depth)
+    ]
+    total = column[0].astype(wide)
+    for k in range(1, grid.depth):
+        total = total + grid.move(column[k], dz=-k).astype(wide)
+    return total
 
 
 def matmul(left, right):
@@ -123,7 +259,36 @@
     )
 
 
+def gather_norms(rows):
+    held = rows.shape[1]
+    count = lax.axis_size(ALL)
+    spread = jnp.zeros((8, held * count), jnp.float32)
+    spread = lax.dynamic_update_slice(spread, rows, (0, lax.axis_index(ALL) * held))
+    return lax.psum(spread, ALL)
+
+
+def sum_norms(terms_of):
+    held = terms_of.shape[1] // lax.axis_size(ALL)
+    total = lax.psum(jnp.pad(terms_of, ((0, 2), (0, 0))), ALL)
+    return lax.dynamic_slice(total, (0, lax.axis_index(ALL) * held), (8, held))
+
+
+def whole_of(grid, place, rows):
+    if not grid.fast:
+        return lax.all_gather(rows, ALL, axis=rows.ndim - 2, tiled=True)
+    return assemble(grid, place, collect(grid, rows))
+
+
+def summed(grid, place, left, right):
+    if not grid.fast:
+        return lax.psum_scatter(across(left, right), ALL, scatter_dimension=0, tiled=True)
+    left_far = grid.move(left, dc=1)
+    right_far = grid.move(right, dc=1)
+    return settle(grid, terms(grid, place, left, left_far, right, right_far, 512))
+
+
 def per_device(
+    grid,
     tokens,
     memory,
     target_segments,
@@ -146,23 +311,16 @@
     final_shift,
     output_grad,
 ):
-    attention_rows = jnp.stack(
-        [
-            self_query,
-            self_key,
-            self_value,
-            self_output,
-            cross_query,
-            cross_key,
-            cross_value,
-            cross_output,
-        ]
-    )
     norm_rows = jnp.stack([self_gain, self_shift, cross_gain, cross_shift, final_gain, final_shift])
-    matrices, expand_full, reduce_full, norm_full = fetch(
-        attention_rows, expand_weight, reduce_weight, norm_rows
-    )
-    gains = norm_full.astype(jnp.float32)
+    place = grid.place()
+    gains = gather_norms(norm_rows.astype(jnp.float32))
+    first_rows = jnp.stack([self_query, self_key, self_value, self_output])
+    second_rows = jnp.stack([cross_query, cross_key, cross_value, cross_output])
+    matrices_one = whole_of(grid, place, first_rows)
+    matrices_two = whole_of(grid, place, second_rows)
+    expand_full = whole_of(grid, place, expand_weight)
+    reduce_full = whole_of(grid, place, reduce_weight)
+    matrices = [matrices_one[i] for i in range(4)] + [matrices_two[i] for i in range(4)]
     target_ids = target_segments[0]
     source_ids = source_segments[0]
     positions = lax.iota(jnp.int32, tokens.shape[0])
@@ -195,62 +353,46 @@
         RESIDUAL_SCALE * second + branch_three, gains[4], gains[5]
     )
     output = final.astype(jnp.bfloat16)
-    matrices, expand_full, reduce_full, norm_full = fetch(
-        attention_rows, expand_weight, reduce_weight, norm_rows
-    )
-    gains = norm_full.astype(jnp.float32)
     d_sum_three, final_gain_term, final_shift_term = normalize_back(
         output_grad.astype(jnp.float32), final_scaled, final_inverse, gains[4]
     )
     d_branch_three = d_sum_three.astype(jnp.bfloat16)
-    reduce_term = across(active, d_branch_three)
+    reduce_term = summed(grid, place, active, d_branch_three)
     d_active = against(d_branch_three, reduce_full)
     d_inner = jax.vjp(gelu_tanh, inner)[1](d_active)[0].astype(jnp.bfloat16)
-    expand_term = across(second_low, d_inner)
+    expand_term = summed(grid, place, second_low, d_inner)
     d_second = RESIDUAL_SCALE * d_sum_three + against(d_inner, expand_full)
     d_sum_two, cross_gain_term, cross_shift_term = normalize_back(
         d_second, second_scaled, second_inverse, gains[2]
     )
     d_branch_two = d_sum_two.astype(jnp.bfloat16)
-    cross_output_term = across(context_two, d_branch_two)
+    cross_output_term = summed(grid, place, context_two, d_branch_two)
     d_context_two = against(d_branch_two, matrices[7]).astype(jnp.bfloat16)
     d_query_two, d_key_two, d_value_two = attend_back(
         query_two, key_two, value_two, crossing, logsum_two, d_context_two
     )
-    cross_query_term = across(first_low, d_query_two)
-    cross_key_term = across(memory, d_key_two)
-    cross_value_term = across(memory, d_value_two)
+    cross_query_term = summed(grid, place, first_low, d_query_two)
+    cross_key_term = summed(grid, place, memory, d_key_two)
+    cross_value_term = summed(grid, place, memory, d_value_two)
     memory_grad = against(d_key_two, matrices[5]) + against(d_value_two, matrices[6])
     d_first = RESIDUAL_SCALE * d_sum_two + against(d_query_two, matrices[4])
     d_sum_one, self_gain_term, self_shift_term = normalize_back(
         d_first, first_scaled, first_inverse, gains[0]
     )
     d_branch_one = d_sum_one.astype(jnp.bfloat16)
-    self_output_term = across(context_one, d_branch_one)
+    self_output_term = summed(grid, place, context_one, d_branch_one)
     d_context_one = against(d_branch_one, matrices[3]).astype(jnp.bfloat16)
     d_query_one, d_key_one, d_value_one = attend_back(
         query_one, key_one, value_one, causal, logsum_one, d_context_one
     )
-    self_query_term = across(tokens, d_query_one)
-    self_key_term = across(tokens, d_key_one)
-    self_value_term = across(tokens, d_value_one)
+    self_query_term = summed(grid, place, tokens, d_query_one)
+    self_key_term = summed(grid, place, tokens, d_key_one)
+    self_value_term = summed(grid, place, tokens, d_value_one)
     tokens_grad = (
         RESIDUAL_SCALE * d_sum_one
         + against(d_query_one, matrices[0])
         + against(d_key_one, matrices[1])
         + against(d_value_one, matrices[2])
-    )
-    attention_terms = jnp.stack(
-        [
-            self_query_term,
-            self_key_term,
-            self_value_term,
-            self_output_term,
-            cross_query_term,
-            cross_key_term,
-            cross_value_term,
-            cross_output_term,
-        ]
     )
     norm_terms = jnp.stack(
         [
@@ -262,23 +404,21 @@
             final_shift_term,
         ]
     )
-    attention_owned, expand_owned, reduce_owned, norm_owned = settle(
-        attention_terms, expand_term, reduce_term, norm_terms
-    )
+    norm_owned = sum_norms(norm_terms)
     return (
         output,
         tokens_grad,
         memory_grad,
-        attention_owned[0],
-        attention_owned[1],
-        attention_owned[2],
-        attention_owned[3],
-        attention_owned[4],
-        attention_owned[5],
-        attention_owned[6],
-        attention_owned[7],
-        expand_owned,
-        reduce_owned,
+        self_query_term,
+        self_key_term,
+        self_value_term,
+        self_output_term,
+        cross_query_term,
+        cross_key_term,
+        cross_value_term,
+        cross_output_term,
+        expand_term,
+        reduce_term,
         norm_owned[0],
         norm_owned[1],
         norm_owned[2],
@@ -290,7 +430,7 @@
 
 def solution(mesh):
     return jax.shard_map(
-        per_device,
+        functools.partial(per_device, Grid(mesh)),
         mesh=mesh,
         in_specs=(
             P(("dp", "fsdp"), None),

time: 1920 us -> 1670 us (0.87)
  waiting for transfers between devices: 1620 us -> 218 us
  Pallas kernels: 0 us -> 1050 us
  starting transfers between devices: 0.67 us -> 142 us
  matrix products: 134 us -> 84.5 us
  local copies, waits for them, and re-layouts: 67.2 us -> 40 us
  other arithmetic: 6.86 us -> 30.9 us
  blocking collectives: 71.5 us -> 90.8 us
    reduce_scatter x3 -> x0, waiting for transfers between devices: 1410 us -> none  [the longest x1 702 us: settle(): lax.psum_scatter(attention_terms, ('dp', 'fsdp'), scatter_dimension=1, ti...]
    pallas_call x0 -> x14, Pallas kernels: none -> 1050 us  [the longest x4 1020 us: assemble(): pl.pallas_call(functools.partial(assemble_kernel, spots, grid.depth, rows...]
    ppermute x0 -> x135, waiting for transfers between devices: none -> 218 us  [move(): return lax.ppermute(value, ALL, pairs)]
    all_gather x3 -> x0, waiting for transfers between devices: 162 us -> none  [the longest x1 71 us: fetch(): lax.all_gather(reduce_rows, ('dp', 'fsdp'), axis=0, tiled=True)]
    ppermute x0 -> x135, starting transfers between devices: none -> 142 us  [move(): return lax.ppermute(value, ALL, pairs)]
    psum x0 -> x2, blocking collectives: none -> 90.8 us  [the longest x1 52.7 us: gather_norms(): return lax.psum(spread, ALL)]
    all_gather x1 -> x0, blocking collectives: 71.5 us -> none  [fetch(): lax.all_gather(norm_rows, ('dp', 'fsdp'), axis=1, tiled=True)]
    dot_general x10 -> x0, matrix products: 42.5 us -> none  [across(): jnp.einsum('ti,tj->ij', left, right, preferred_element_type=jnp.float32)]
  transfers between devices with their start and end apart: 7 -> 135, of which waited for: 7 -> 48; matrix products, arithmetic and copies ran while one was open for 7% -> 9% of each run, Pallas kernels for 0% -> 63%
where the time goes in v1:
time: 1670 us; the launch traced here: 1660 us
  Pallas kernels  1050 us (63%)
  waiting for transfers between devices  218 us (13%)
  starting transfers between devices  142 us (9%)
  blocking collectives  90.8 us (5%)
  matrix products  84.5 us (5%)
  local copies, waits for them, and re-layouts  40 us (2%)
  other arithmetic  30.9 us (2%)
    pallas_call x4, Pallas kernels, assemble(): pl.pallas_call(functools.partial(assemble_kernel, spots, grid.depth, rows...  1020 us
    ppermute x135, waiting for transfers between devices, move(): return lax.ppermute(value, ALL, pairs)  218 us
    ppermute x135, starting transfers between devices, move(): return lax.ppermute(value, ALL, pairs)  142 us
    psum x1, blocking collectives, gather_norms(): return lax.psum(spread, ALL)  52.7 us
    psum x1, blocking collectives, sum_norms(): total = lax.psum(jnp.pad(terms_of, ((0, 2), (0, 0))), ALL)  38.1 us
    dot_general x10, matrix products, against(): jnp.einsum('ti,ji->tj', left, right, preferred_element_type=jnp.float32)  35.4 us
  transfers between devices with their start and end apart: 135, of which 48 were waited for; matrix products, arithmetic and copies ran while one was open for 9% of the time, Pallas kernels for 63%

profile of v1, /device:TPU:0, one launch (start us, length us, event | category | flops | bytes accessed | tf_op | source)
XLA Modules:
  0.0 1660.8 jit_solution(9721339584603846363)
XLA Ops:
  12.1 7.4 collective-permute-done.13
  19.5 8.7 collective-permute-start
  35.1 17.2 %collective-permute-done.1 = bf16[4,32,1024]{2,1,0:T(8,128)(2,1)S(1)} collective-permute-done((bf16[4,32,1024]{2,1,0:T(8,128)(2,1)S(1)}, bf16[4,32,1024]{2,1,0:T(8,128)(2,1)S(1)}, u32[]{:S(2)}, u32[]{:S(2)}) %collective-permute-start.1) | collective-permute-done | bytes 262176 | tf_op jit(solution)/shard_map/ppermute | solution.py:37
  56.2 6.3 collective-permute-start.38
  65.8 8.2 collective-permute-done.36
  76.6 17.8 %collective-permute-done.37 = bf16[128,1024]{1,0:T(8,128)(2,1)S(1)} collective-permute-done((bf16[128,1024]{1,0:T(8,128)(2,1)S(1)}, bf16[128,1024]{1,0:T(8,128)(2,1)S(1)}, u32[]{:S(2)}, u32[]{:S(2)}) %collective-permute-start.37) | collective-permute-done | bytes 262176 | tf_op jit(solution)/shard_map/ppermute | solution.py:37
  95.6 7.8 collective-permute-done.25
  114.4 15.3 collective-permute-done.40.refs_2_
  131.7 20.4 %collective-permute-done.28.refs_2_ = bf16[4,32,4096]{2,1,0:T(8,128)(2,1)} collective-permute-done((bf16[4,32,4096]{2,1,0:T(8,128)(2,1)}, bf16[4,32,4096]{2,1,0:T(8,128)(2,1)}, u32[]{:S(2)}, u32[]{:S(2)}) %collective-permute-start.28) | collective-permute-done | bytes 1048608 | tf_op jit(solution)/shard_map/ppermute | solution.py:37
  154.3 52.7 %psum.14 = f32[8,1024]{1,0:T(8,128)S(1)} all-reduce(f32[8,1024]{1,0:T(8,128)S(1)} %dynamic_update_slice.3), channel_id=1, replica_groups=mesh['dp'=8,'fsdp'=4] {'dp','fsdp'}, use_global_device_ids=true, to_apply=%region_4.5 | all-reduce | flops 8192 | bytes 65536 | tf_op jit(solution)/shard_map/psum | solution.py:267
  223.7 256.2 %assemble.4 = bf16[4,1024,1024]{2,1,0:T(8,128)(2,1)} custom-call(s32[4]{0:T(128)} %pad_add_fusion.place, bf16[4,4,32,1024]{3,2,1,0:T(8,128)(2,1)} %copy-done.38, bf16[4,4,32,1024]{3,2,1,0:T(8,128)(2,1)} %collective-permute-done.3.refs_1_, bf16[4,4,32,1024]{3,2,1,0:T(8,128)(2,1)} %collective-permute-done.4.refs_2_, ...), custom_call_target="tpu_custom_call" | custom-call | bytes 16777216 | tf_op jit(solution)/shard_map/assemble/pallas_call | solution.py:76
  494.2 256.2 %assemble.5 = bf16[4,1024,1024]{2,1,0:T(8,128)(2,1)} custom-call(s32[4]{0:T(128)} %pad_add_fusion.place, bf16[4,4,32,1024]{3,2,1,0:T(8,128)(2,1)} %copy-done.37, bf16[4,4,32,1024]{3,2,1,0:T(8,128)(2,1)} %collective-permute-done.15.refs_1_, bf16[4,4,32,1024]{3,2,1,0:T(8,128)(2,1)} %collective-permute-done.16.refs_2_, ...), custom_call_target="tpu_custom_call" | custom-call | bytes 16777216 | tf_op jit(solution)/shard_map/assemble/pallas_call | solution.py:76
  764.7 12.5 collective-permute-done.41.refs_3_
  778.5 256.2 %assemble.6 = bf16[1024,4096]{1,0:T(8,128)(2,1)} custom-call(s32[4]{0:T(128)} %pad_add_fusion.place, bf16[4,32,4096]{2,1,0:T(8,128)(2,1)} %pad_maximum_fusion.2.refs_0_, bf16[4,32,4096]{2,1,0:T(8,128)(2,1)} %collective-permute-done.27.refs_1_, bf16[4,32,4096]{2,1,0:T(8,128)(2,1)} %collective-permute-done.28.refs_2_, ...), custom_call_target="tpu_custom_call" | custom-call | bytes 16777216 | tf_op jit(solution)/shard_map/assemble/pallas_call | solution.py:76
  1034.7 9.2 multiply_convert_fusion.1
  1044.8 256.2 %assemble.7 = bf16[4096,1024]{1,0:T(8,128)(2,1)} custom-call(s32[4]{0:T(128)} %pad_add_fusion.place, bf16[4,128,1024]{2,1,0:T(8,128)(2,1)} %pad_maximum_fusion.3.refs_0_, bf16[4,128,1024]{2,1,0:T(8,128)(2,1)} %collective-permute-done.39.refs_1_, bf16[4,128,1024]{2,1,0:T(8,128)(2,1)} %collective-permute-done.40.refs_2_, ...), custom_call_target="tpu_custom_call" | custom-call | bytes 16777216 | tf_op jit(solution)/shard_map/assemble/pallas_call | solution.py:76
  1301.0 6.6 fusion.136
  1309.8 8.6 fusion.6.right
  1371.3 38.1 %psum.15 = f32[8,1024]{1,0:T(8,128)S(1)} all-reduce(f32[8,1024]{1,0:T(8,128)S(1)} %pad.44), channel_id=1, replica_groups=mesh['dp'=8,'fsdp'=4] {'dp','fsdp'}, use_global_device_ids=true, to_apply=%region_25.26 | all-reduce | flops 8192 | bytes 65536 | tf_op jit(solution)/shard_map/psum | solution.py:272
  1571.8 9.8 collective-permute-done.121
  1609.4 5.1 collective-permute-done.122
  1614.5 7.1 collective-permute-done.120
  1625.9 7.0 collective-permute-done.129
  1637.7 15.9 collective-permute-done.124
  (553 shorter events, 351.6 us)
Async XLA Ops:
  31.4 72.0 %collective-permute-start.16 = (bf16[4,4,32,1024]{3,2,1,0:T(8,128)(2,1)S(1)}, bf16[4,4,32,1024]{3,2,1,0:T(8,128)(2,1)}, u32[]{:S(2)}, u32[]{:S(2)}) collective-permute-start(bf16[4,4,32,1024]{3,2,1,0:T(8,128)(2,1)S(1)} %pad_maximum_fusion.1.refs_0_), channel_id=1, source_target_pairs={{2,0},{3,1},{0,2},{1,3},{6,4},{7,5},{4,6},{5,7},{10,8},{11,9},{8,1... | collective-permute-start | bytes 3145736 | tf_op jit(solution)/shard_map/ppermute | solution.py:37
  33.6 71.3 %collective-permute-start.15 = (bf16[4,4,32,1024]{3,2,1,0:T(8,128)(2,1)S(1)}, bf16[4,4,32,1024]{3,2,1,0:T(8,128)(2,1)}, u32[]{:S(2)}, u32[]{:S(2)}) collective-permute-start(bf16[4,4,32,1024]{3,2,1,0:T(8,128)(2,1)S(1)} %pad_maximum_fusion.1.refs_0_), channel_id=1, source_target_pairs={{1,0},{0,1},{3,2},{2,3},{5,4},{4,5},{7,6},{6,7},{9,8},{8,9},{11,10... | collective-permute-start | bytes 3145736 | tf_op jit(solution)/shard_map/ppermute | solution.py:37
  114.4 93.8 %collective-permute-start.18 = (bf16[2,4,32,1024]{3,2,1,0:T(8,128)(2,1)}, bf16[2,4,32,1024]{3,2,1,0:T(8,128)(2,1)}, u32[]{:S(2)}, u32[]{:S(2)}) collective-permute-start(bf16[2,4,32,1024]{3,2,1,0:T(8,128)(2,1)} %slice.1104), channel_id=1, source_target_pairs={{1,0},{0,1},{3,2},{2,3},{5,4},{4,5},{7,6},{6,7},{9,8},{8,9},{11,10... | collective-permute-start | bytes 1572872 | tf_op jit(solution)/shard_map/ppermute | solution.py:37
  129.7 80.9 %collective-permute-start.6 = (bf16[2,4,32,1024]{3,2,1,0:T(8,128)(2,1)}, bf16[2,4,32,1024]{3,2,1,0:T(8,128)(2,1)S(1)}, u32[]{:S(2)}, u32[]{:S(2)}) collective-permute-start(bf16[2,4,32,1024]{3,2,1,0:T(8,128)(2,1)} %slice.1096), channel_id=1, source_target_pairs={{1,0},{0,1},{3,2},{2,3},{5,4},{4,5},{7,6},{6,7},{9,8},{8,9},{11,10... | collective-permute-start | bytes 1572872 | tf_op jit(solution)/shard_map/ppermute | solution.py:37
  131.2 79.4 %collective-permute-start.5 = (bf16[2,4,32,1024]{3,2,1,0:T(8,128)(2,1)S(1)}, bf16[2,4,32,1024]{3,2,1,0:T(8,128)(2,1)}, u32[]{:S(2)}, u32[]{:S(2)}) collective-permute-start(bf16[2,4,32,1024]{3,2,1,0:T(8,128)(2,1)S(1)} %slice.1095), channel_id=1, source_target_pairs={{2,0},{3,1},{0,2},{1,3},{6,4},{7,5},{4,6},{5,7},{10,8},{11,9},{8,1... | collective-permute-start | bytes 1572872 | tf_op jit(solution)/shard_map/ppermute | solution.py:37
  152.1 69.7 %collective-permute-start.9 = (bf16[4,4,32,1024]{3,2,1,0:T(8,128)(2,1)}, bf16[4,4,32,1024]{3,2,1,0:T(8,128)(2,1)}, u32[]{:S(2)}, u32[]{:S(2)}) collective-permute-start(bf16[4,4,32,1024]{3,2,1,0:T(8,128)(2,1)} %collective-permute-done.4.refs_2_), channel_id=1, source_target_pairs={{4,0},{5,1},{6,2},{7,3},{0,4},{1,5},{2,6},{3,7},{12,8},{13,9},{14,... | collective-permute-start | bytes 3145736 | tf_op jit(solution)/shard_map/ppermute | solution.py:37
  221.8 268.4 %collective-permute-start.19 = (bf16[4,4,32,1024]{3,2,1,0:T(8,128)(2,1)S(1)}, bf16[4,4,32,1024]{3,2,1,0:T(8,128)(2,1)}, u32[]{:S(2)}, u32[]{:S(2)}) collective-permute-start(bf16[4,4,32,1024]{3,2,1,0:T(8,128)(2,1)S(1)} %pad_maximum_fusion.1.refs_0_), channel_id=1, source_target_pairs={{4,0},{5,1},{6,2},{7,3},{0,4},{1,5},{2,6},{3,7},{12,8},{13,9},{14,... | collective-permute-start | bytes 3145736 | tf_op jit(solution)/shard_map/ppermute | solution.py:37
  221.8 268.6 %collective-permute-start.21 = (bf16[4,4,32,1024]{3,2,1,0:T(8,128)(2,1)}, bf16[4,4,32,1024]{3,2,1,0:T(8,128)(2,1)}, u32[]{:S(2)}, u32[]{:S(2)}) collective-permute-start(bf16[4,4,32,1024]{3,2,1,0:T(8,128)(2,1)} %collective-permute-done.16.refs_2_), channel_id=1, source_target_pairs={{4,0},{5,1},{6,2},{7,3},{0,4},{1,5},{2,6},{3,7},{12,8},{13,9},{14,... | collective-permute-start | bytes 3145736 | tf_op jit(solution)/shard_map/ppermute | solution.py:37
  222.4 269.8 %collective-permute-start.20 = (bf16[4,4,32,1024]{3,2,1,0:T(8,128)(2,1)}, bf16[4,4,32,1024]{3,2,1,0:T(8,128)(2,1)}, u32[]{:S(2)}, u32[]{:S(2)}) collective-permute-start(bf16[4,4,32,1024]{3,2,1,0:T(8,128)(2,1)} %collective-permute-done.15.refs_1_), channel_id=1, source_target_pairs={{4,0},{5,1},{6,2},{7,3},{0,4},{1,5},{2,6},{3,7},{12,8},{13,9},{14,... | collective-permute-start | bytes 3145736 | tf_op jit(solution)/shard_map/ppermute | solution.py:37
  222.4 270.0 %collective-permute-start.23 = (bf16[2,4,32,1024]{3,2,1,0:T(8,128)(2,1)}, bf16[2,4,32,1024]{3,2,1,0:T(8,128)(2,1)}, u32[]{:S(2)}, u32[]{:S(2)}) collective-permute-start(bf16[2,4,32,1024]{3,2,1,0:T(8,128)(2,1)} %collective-permute-done.18.refs_4_), channel_id=1, source_target_pairs={{4,0},{5,1},{6,2},{7,3},{0,4},{1,5},{2,6},{3,7},{12,8},{13,9},{14,... | collective-permute-start | bytes 1572872 | tf_op jit(solution)/shard_map/ppermute | solution.py:37
  222.9 271.4 %collective-permute-start.22 = (bf16[2,4,32,1024]{3,2,1,0:T(8,128)(2,1)}, bf16[2,4,32,1024]{3,2,1,0:T(8,128)(2,1)}, u32[]{:S(2)}, u32[]{:S(2)}) collective-permute-start(bf16[2,4,32,1024]{3,2,1,0:T(8,128)(2,1)} %collective-permute-done.17.refs_3_), channel_id=1, source_target_pairs={{4,0},{5,1},{6,2},{7,3},{0,4},{1,5},{2,6},{3,7},{12,8},{13,9},{14,... | collective-permute-start | bytes 1572872 | tf_op jit(solution)/shard_map/ppermute | solution.py:37
  490.2 269.6 %collective-permute-start.31 = (bf16[4,32,4096]{2,1,0:T(8,128)(2,1)}, bf16[4,32,4096]{2,1,0:T(8,128)(2,1)}, u32[]{:S(2)}, u32[]{:S(2)}) collective-permute-start(bf16[4,32,4096]{2,1,0:T(8,128)(2,1)} %pad_maximum_fusion.2.refs_0_), channel_id=1, source_target_pairs={{4,0},{5,1},{6,2},{7,3},{0,4},{1,5},{2,6},{3,7},{12,8},{13,9},{14,... | collective-permute-start | bytes 3145736 | tf_op jit(solution)/shard_map/ppermute | solution.py:37
  490.4 272.5 %collective-permute-start.42 = (bf16[2,128,1024]{2,1,0:T(8,128)(2,1)}, bf16[2,128,1024]{2,1,0:T(8,128)(2,1)}, u32[]{:S(2)}, u32[]{:S(2)}) collective-permute-start(bf16[2,128,1024]{2,1,0:T(8,128)(2,1)} %slice.1114), channel_id=1, source_target_pairs={{1,0},{0,1},{3,2},{2,3},{5,4},{4,5},{7,6},{6,7},{9,8},{8,9},{11,10... | collective-permute-start | bytes 1572872 | tf_op jit(solution)/shard_map/ppermute | solution.py:37
  492.1 271.1 %collective-permute-start.30 = (bf16[2,32,4096]{2,1,0:T(8,128)(2,1)}, bf16[2,32,4096]{2,1,0:T(8,128)(2,1)}, u32[]{:S(2)}, u32[]{:S(2)}) collective-permute-start(bf16[2,32,4096]{2,1,0:T(8,128)(2,1)} %slice.1112), channel_id=1, source_target_pairs={{1,0},{0,1},{3,2},{2,3},{5,4},{4,5},{7,6},{6,7},{9,8},{8,9},{11,10... | collective-permute-start | bytes 1572872 | tf_op jit(solution)/shard_map/ppermute | solution.py:37
  492.5 270.8 %collective-permute-start.29 = (bf16[2,32,4096]{2,1,0:T(8,128)(2,1)}, bf16[2,32,4096]{2,1,0:T(8,128)(2,1)}, u32[]{:S(2)}, u32[]{:S(2)}) collective-permute-start(bf16[2,32,4096]{2,1,0:T(8,128)(2,1)} %slice.1111), channel_id=1, source_target_pairs={{2,0},{3,1},{0,2},{1,3},{6,4},{7,5},{4,6},{5,7},{10,8},{11,9},{8,1... | collective-permute-start | bytes 1572872 | tf_op jit(solution)/shard_map/ppermute | solution.py:37
  494.2 282.9 %collective-permute-start.33 = (bf16[4,32,4096]{2,1,0:T(8,128)(2,1)}, bf16[4,32,4096]{2,1,0:T(8,128)(2,1)}, u32[]{:S(2)}, u32[]{:S(2)}) collective-permute-start(bf16[4,32,4096]{2,1,0:T(8,128)(2,1)} %collective-permute-done.28.refs_2_), channel_id=1, source_target_pairs={{4,0},{5,1},{6,2},{7,3},{0,4},{1,5},{2,6},{3,7},{12,8},{13,9},{14,... | collective-permute-start | bytes 3145736 | tf_op jit(solution)/shard_map/ppermute | solution.py:37
  777.2 267.0 %collective-permute-start.43 = (bf16[4,128,1024]{2,1,0:T(8,128)(2,1)}, bf16[4,128,1024]{2,1,0:T(8,128)(2,1)}, u32[]{:S(2)}, u32[]{:S(2)}) collective-permute-start(bf16[4,128,1024]{2,1,0:T(8,128)(2,1)} %pad_maximum_fusion.3.refs_0_), channel_id=1, source_target_pairs={{4,0},{5,1},{6,2},{7,3},{0,4},{1,5},{2,6},{3,7},{12,8},{13,9},{14,... | collective-permute-start | bytes 3145736 | tf_op jit(solution)/shard_map/ppermute | solution.py:37
  777.2 267.5 %collective-permute-start.45 = (bf16[4,128,1024]{2,1,0:T(8,128)(2,1)}, bf16[4,128,1024]{2,1,0:T(8,128)(2,1)}, u32[]{:S(2)}, u32[]{:S(2)}) collective-permute-start(bf16[4,128,1024]{2,1,0:T(8,128)(2,1)} %collective-permute-done.40.refs_2_), channel_id=1, source_target_pairs={{4,0},{5,1},{6,2},{7,3},{0,4},{1,5},{2,6},{3,7},{12,8},{13,9},{14,... | collective-permute-start | bytes 3145736 | tf_op jit(solution)/shard_map/ppermute | solution.py:37
  777.7 267.1 %collective-permute-start.44 = (bf16[4,128,1024]{2,1,0:T(8,128)(2,1)}, bf16[4,128,1024]{2,1,0:T(8,128)(2,1)}, u32[]{:S(2)}, u32[]{:S(2)}) collective-permute-start(bf16[4,128,1024]{2,1,0:T(8,128)(2,1)} %collective-permute-done.39.refs_1_), channel_id=1, source_target_pairs={{4,0},{5,1},{6,2},{7,3},{0,4},{1,5},{2,6},{3,7},{12,8},{13,9},{14,... | collective-permute-start | bytes 3145736 | tf_op jit(solution)/shard_map/ppermute | solution.py:37
  777.8 267.0 %collective-permute-start.47 = (bf16[2,128,1024]{2,1,0:T(8,128)(2,1)}, bf16[2,128,1024]{2,1,0:T(8,128)(2,1)}, u32[]{:S(2)}, u32[]{:S(2)}) collective-permute-start(bf16[2,128,1024]{2,1,0:T(8,128)(2,1)} %collective-permute-done.42.refs_4_), channel_id=1, source_target_pairs={{4,0},{5,1},{6,2},{7,3},{0,4},{1,5},{2,6},{3,7},{12,8},{13,9},{14,... | collective-permute-start | bytes 1572872 | tf_op jit(solution)/shard_map/ppermute | solution.py:37
  778.3 266.5 %collective-permute-start.46 = (bf16[2,128,1024]{2,1,0:T(8,128)(2,1)}, bf16[2,128,1024]{2,1,0:T(8,128)(2,1)}, u32[]{:S(2)}, u32[]{:S(2)}) collective-permute-start(bf16[2,128,1024]{2,1,0:T(8,128)(2,1)} %collective-permute-done.41.refs_3_), channel_id=1, source_target_pairs={{4,0},{5,1},{6,2},{7,3},{0,4},{1,5},{2,6},{3,7},{12,8},{13,9},{14,... | collective-permute-start | bytes 1572872 | tf_op jit(solution)/shard_map/ppermute | solution.py:37
  1044.2 365.2 %collective-permute-start.91 = (bf16[128,1024]{1,0:T(8,128)(2,1)}, bf16[128,1024]{1,0:T(8,128)(2,1)}, u32[]{:S(2)}, u32[]{:S(2)}) collective-permute-start(bf16[128,1024]{1,0:T(8,128)(2,1)} %left.9), channel_id=1, source_target_pairs={{4,0},{5,1},{6,2},{7,3},{0,4},{1,5},{2,6},{3,7},{12,8},{13,9},{14,... | collective-permute-start | bytes 786440 | tf_op jit(solution)/shard_map/ppermute | solution.py:37
  1044.7 381.1 %collective-permute-start.48 = (bf16[256,1024]{1,0:T(8,128)(2,1)S(1)}, bf16[256,1024]{1,0:T(8,128)(2,1)S(1)}, u32[]{:S(2)}, u32[]{:S(2)}) collective-permute-start(bf16[256,1024]{1,0:T(8,128)(2,1)S(1)} %copy-done), channel_id=1, source_target_pairs={{4,0},{5,1},{6,2},{7,3},{0,4},{1,5},{2,6},{3,7},{12,8},{13,9},{14,... | collective-permute-start | bytes 1572872 | tf_op jit(solution)/shard_map/ppermute | solution.py:37
  1353.7 87.1 %collective-permute-start.73 = (bf16[256,1024]{1,0:T(8,128)(2,1)S(1)}, bf16[256,1024]{1,0:T(8,128)(2,1)}, u32[]{:S(2)}, u32[]{:S(2)}) collective-permute-start(bf16[256,1024]{1,0:T(8,128)(2,1)S(1)} %copy.80.left), channel_id=1, source_target_pairs={{4,0},{5,1},{6,2},{7,3},{0,4},{1,5},{2,6},{3,7},{12,8},{13,9},{14,... | collective-permute-start | bytes 1572872 | tf_op jit(solution)/shard_map/ppermute | solution.py:37
  (188 other events, 5353.8 us)

commit v2 on v0

--- a/solution.py
+++ b/solution.py
@@ -1,6 +1,10 @@
+import functools
+
 import jax
 import jax.numpy as jnp
 from jax import lax
+from jax.experimental import pallas as pl
+from jax.experimental.pallas import tpu as pltpu
 from jax.sharding import PartitionSpec as P
 
 HEADS = 16
@@ -10,6 +14,658 @@
 RESIDUAL_SCALE = 300.0**0.25
 EPSILON = 1e-05
 NEGATIVE = -1e30
+ALL = ("dp", "fsdp")
+
+
+class Grid:
+    def __init__(self, mesh):
+        self.depth = mesh.shape["dp"] // 2
+        self.count = mesh.size
+        self.fast = mesh.shape["fsdp"] == 4 and mesh.shape["dp"] == 8
+
+    def place(self):
+        index = lax.axis_index(ALL)
+        return jnp.stack([index // 8, index // 4 % 2, index // 2 % 2, index % 2]).astype(jnp.int32)
+
+    def move(self, value, dz=0, dc=0, dy=0, dx=0):
+        offset = ((dz * 2 + dc) * 2 + dy) * 2 + dx
+        return lax.ppermute(value, ALL, [(index ^ offset, index) for index in range(self.count)])
+
+
+def after(value, *others):
+    return lax.optimization_barrier((value,) + others)[0]
+
+
+def gather_direct(grid, shard):
+    return jnp.stack([shard] + [grid.move(shard, dz=k) for k in range(1, grid.depth)])
+
+
+def gather_pair(grid, shard):
+    return jnp.stack([shard, grid.move(shard, dz=1)])
+
+
+def gather_pairs(grid, pair):
+    return jnp.concatenate([pair, grid.move(pair, dz=2)])
+
+
+def gather_sides(grid, own):
+    return grid.move(own, dx=1), grid.move(own, dy=1)
+
+
+def gather_corner(grid, own, sides):
+    half = grid.depth // 2
+    low = grid.move(sides[0][:half], dy=1)
+    high = grid.move(sides[1][half:], dx=1)
+    far = grid.move(jnp.concatenate([own, *sides]), dc=1)
+    return low, high, far
+
+
+def gather_last(grid, low, high):
+    corner = jnp.concatenate([low, high])
+    return corner, grid.move(corner, dc=1)
+
+
+def wide_dot(left, right):
+    return jnp.dot(left, right, preferred_element_type=jnp.float32)
+
+
+def dot_rows(left, right):
+    return lax.dot_general(left, right, (((1,), (1,)), ((), ())), preferred_element_type=jnp.float32)
+
+
+def dot_columns(left, right):
+    return lax.dot_general(left, right, (((0,), (0,)), ((), ())), preferred_element_type=jnp.float32)
+
+
+def whole_call(body, name, inputs, shapes, scratch=(), limit=56):
+    arrays, specs = [], []
+    for item in inputs:
+        if not isinstance(item, tuple):
+            item = (item, item.shape, (0,) * item.ndim)
+        arrays.append(item[0])
+        if len(item) == 2:
+            specs.append(pl.BlockSpec(memory_space=item[1]))
+        else:
+            specs.append(pl.BlockSpec(item[1], lambda i, index=item[2]: index))
+    outs, out_specs = [], []
+    for item in shapes:
+        outs.append(jax.ShapeDtypeStruct(item[0], item[1]))
+        if len(item) == 3:
+            out_specs.append(pl.BlockSpec(memory_space=item[2]))
+        else:
+            out_specs.append(pl.BlockSpec(item[0], lambda i, rank=len(item[0]): (0,) * rank))
+    return pl.pallas_call(
+        body,
+        grid=(1,),
+        out_shape=outs,
+        in_specs=specs,
+        out_specs=out_specs,
+        scratch_shapes=list(scratch),
+        compiler_params=pltpu.CompilerParams(vmem_limit_bytes=limit * 2**20),
+        cost_estimate=pl.CostEstimate(flops=1, bytes_accessed=1, transcendentals=0),
+        name=name,
+    )(*arrays)
+
+
+def arrivals_of(depth, rows, place, pieces, held, sems, held_norms=None):
+    own, over_x, over_y, far, corner, corner_far = pieces
+    z, c, y, x = place[0], place[1], place[2], place[3]
+    width = held.shape[-1]
+    arrivals = []
+    for k in range(depth):
+        column = []
+        for n in range(8):
+            dc, dy, dx = n // 4, n // 2 % 2, n % 2
+            if n % 4 == 3:
+                piece, spot = (corner_far if dc else corner), k
+            elif dc:
+                piece, spot = far, (n % 4) * depth + k
+            else:
+                piece, spot = (own, over_x, over_y)[n], k
+            owner = (((z ^ k) * 2 + (c ^ dc)) * 2 + (y ^ dy)) * 2 + (x ^ dx)
+            target = held.at[..., pl.ds(pl.multiple_of(owner * rows, rows), rows), :]
+            source = piece.at[spot]
+            order = k * 8 + n
+            if held_norms is None:
+                column.append(pltpu.make_async_copy(source, target, sems.at[order]))
+            else:
+                column.append(pltpu.make_async_copy(source.at[..., :width], target, sems.at[order]))
+                column.append(
+                    pltpu.make_async_copy(
+                        source.at[0:2, :, pl.ds(width, 128)],
+                        held_norms.at[owner],
+                        sems.at[8 * depth + order],
+                    )
+                )
+        for copy in column:
+            copy.start()
+        arrivals.append(column)
+    return arrivals
+
+
+def pass_on(depth, rows, place, arrivals, held, whole, sems):
+    leaving = []
+    for k in range(depth):
+        for copy in arrivals[k]:
+            copy.wait()
+        spot = pl.ds(pl.multiple_of((place[0] ^ k) * (8 * rows), 8 * rows), 8 * rows)
+        leaving.append(pltpu.make_async_copy(held.at[..., spot, :], whole.at[..., spot, :], sems.at[k]))
+        leaving[k].start()
+    return leaving
+
+
+def norm_rows_of(summed, gain, shift):
+    center = jnp.mean(summed, axis=-1, keepdims=True)
+    centred = summed - center
+    inverse = lax.rsqrt(jnp.mean(centred * centred, axis=-1, keepdims=True) + EPSILON)
+    scaled = centred * inverse
+    return scaled * gain + shift, scaled, inverse
+
+
+def norm_rows_back(incoming, scaled, inverse, gain):
+    spread_out = incoming * gain
+    d_summed = inverse * (
+        spread_out
+        - jnp.mean(spread_out, axis=-1, keepdims=True)
+        - scaled * jnp.mean(spread_out * scaled, axis=-1, keepdims=True)
+    )
+    return d_summed, jnp.sum(incoming * scaled, axis=0, keepdims=True), jnp.sum(incoming, axis=0, keepdims=True)
+
+
+def head_halves():
+    lane = lax.broadcasted_iota(jnp.int32, (1, 2 * HEAD_DIM), 1)
+    return [
+        jnp.where(lane < HEAD_DIM, 1.0, 0.0).astype(jnp.bfloat16),
+        jnp.where(lane < HEAD_DIM, 0.0, 1.0).astype(jnp.bfloat16),
+    ]
+
+
+def attend_heads(query, key, value, allowed, context, logsum):
+    halves = head_halves()
+    lane = lax.broadcasted_iota(jnp.int32, logsum.shape, 1)
+    logsum[...] = jnp.zeros_like(logsum)
+
+    def pair(p, carry):
+        lanes = pl.ds(pl.multiple_of(p * 2 * HEAD_DIM, 2 * HEAD_DIM), 2 * HEAD_DIM)
+        queries, keys, values = query[:, lanes], key[:, lanes], value[:, lanes]
+        total = None
+        for side, half in enumerate(halves):
+            scores = dot_rows(queries * half, keys) * HEAD_DIM ** (-0.5)
+            scores = jnp.where(allowed[...] > 0, scores, NEGATIVE)
+            highest = jnp.max(scores, axis=-1, keepdims=True)
+            weights = jnp.exp(scores - highest)
+            totals = jnp.sum(weights, axis=-1, keepdims=True)
+            chances = (weights * (1.0 / totals)).astype(jnp.bfloat16)
+            part = wide_dot(chances, values * half)
+            total = part if total is None else total + part
+            logsum[...] = jnp.where(lane == 2 * p + side, highest + jnp.log(totals), logsum[...])
+        context[:, lanes] = total.astype(jnp.bfloat16)
+        return carry
+
+    lax.fori_loop(0, HEADS // 2, pair, 0)
+
+
+def attend_heads_back(query, key, value, allowed, logsum, d_context, d_query, d_key, d_value):
+    halves = head_halves()
+    lane = lax.broadcasted_iota(jnp.int32, logsum.shape, 1)
+    scale = HEAD_DIM ** (-0.5)
+
+    def pair(p, carry):
+        lanes = pl.ds(pl.multiple_of(p * 2 * HEAD_DIM, 2 * HEAD_DIM), 2 * HEAD_DIM)
+        queries, keys, values, d_outs = query[:, lanes], key[:, lanes], value[:, lanes], d_context[:, lanes]
+        sums = [None, None, None]
+        for side, half in enumerate(halves):
+            own_sum = jnp.sum(jnp.where(lane == 2 * p + side, logsum[...], 0.0), axis=-1, keepdims=True)
+            own_queries, own_outs = queries * half, d_outs * half
+            scores = dot_rows(own_queries, keys) * scale
+            scores = jnp.where(allowed[...] > 0, scores, NEGATIVE)
+            chances = jnp.exp(scores - own_sum)
+            d_chances = dot_rows(own_outs, values)
+            centre = jnp.sum(d_chances * chances, axis=-1, keepdims=True)
+            d_scores = (chances * (d_chances - centre)).astype(jnp.bfloat16)
+            parts = (
+                wide_dot(d_scores, keys * half),
+                dot_columns(d_scores, own_queries),
+                dot_columns(chances.astype(jnp.bfloat16), own_outs),
+            )
+            sums = [part if old is None else old + part for old, part in zip(sums, parts)]
+        d_query[:, lanes] = (sums[0] * scale).astype(jnp.bfloat16)
+        d_key[:, lanes] = (sums[1] * scale).astype(jnp.bfloat16)
+        d_value[:, lanes] = sums[2].astype(jnp.bfloat16)
+        return carry
+
+    lax.fori_loop(0, HEADS // 2, pair, 0)
+
+
+def self_allowed(ids_column, ids_row, allowed):
+    rows, columns = allowed.shape
+    later = lax.broadcasted_iota(jnp.int32, (rows, columns), 0) >= lax.broadcasted_iota(
+        jnp.int32, (rows, columns), 1
+    )
+    same = ids_column[...] == ids_row[...]
+    allowed[...] = jnp.where(later & same, 1.0, 0.0)
+
+
+def cross_allowed(ids_column, ids_row, allowed):
+    allowed[...] = jnp.where(ids_column[...] == ids_row[...], 1.0, 0.0)
+
+
+def self_forward_kernel(depth, rows, place, tokens, ids_column, ids_row, *refs):
+    pieces, refs = refs[:6], refs[6:]
+    whole, gains, query, key, value, context, logsum, first, first_low, scaled, inverse = refs[:11]
+    held, held_norms, allowed, in_sems, out_sems = refs[11:]
+    arrivals = arrivals_of(depth, rows, place, pieces, held, in_sems, held_norms)
+    self_allowed(ids_column, ids_row, allowed)
+    leaving = pass_on(depth, rows, place, arrivals, held, whole, out_sems)
+    packed = held_norms[0].astype(jnp.float32)
+    for owner in range(1, 8 * depth):
+        packed += held_norms[owner].astype(jnp.float32)
+    gains[...] = jnp.zeros_like(gains)
+    for n in range(6):
+        for j in range(8):
+            r = n * 8 + j
+            gains[n : n + 1, j * 128 : (j + 1) * 128] = packed[r // rows, r % rows : r % rows + 1, :]
+    for n, out in enumerate((query, key, value)):
+        out[...] = wide_dot(tokens[...], held[n]).astype(jnp.bfloat16)
+    attend_heads(query, key, value, allowed, context, logsum)
+    branch = wide_dot(context[...], held[3])
+    summed = RESIDUAL_SCALE * tokens[...].astype(jnp.float32) + branch
+    first[...], scaled[...], inverse[...] = norm_rows_of(summed, gains[0:1, :], gains[1:2, :])
+    first_low[...] = first[...].astype(jnp.bfloat16)
+    for copy in leaving:
+        copy.wait()
+
+
+def self_forward(grid, place, tokens, ids_column, ids_row, pieces):
+    count, width = tokens.shape
+    rows = pieces[0].shape[2]
+    low, full = jnp.bfloat16, jnp.float32
+    shape = (count, width)
+    return whole_call(
+        functools.partial(self_forward_kernel, grid.depth, rows),
+        "self_forward",
+        [(place, pltpu.SMEM), tokens, ids_column, ids_row] + [(piece, pl.ANY) for piece in pieces],
+        [((4, width, width), low, pl.ANY), ((8, width), full)]
+        + [(shape, low)] * 4
+        + [((count, 128), full), (shape, full), (shape, low), (shape, full), ((count, 1), full)],
+        [
+            pltpu.VMEM((4, width, width), low),
+            pltpu.VMEM((grid.count, 2, rows, 128), low),
+            pltpu.VMEM((count, count), full),
+            pltpu.SemaphoreType.DMA((2 * grid.count,)),
+            pltpu.SemaphoreType.DMA((grid.depth,)),
+        ],
+    )
+
+
+def cross_forward_kernel(depth, rows, place, first, first_low, memory, gains, ids_column, ids_row, *refs):
+    pieces, refs = refs[:6], refs[6:]
+    whole, query, key, value, context, logsum, second, second_low, scaled, inverse = refs[:10]
+    held, allowed, in_sems, out_sems = refs[10:]
+    arrivals = arrivals_of(depth, rows, place, pieces, held, in_sems)
+    cross_allowed(ids_column, ids_row, allowed)
+    leaving = pass_on(depth, rows, place, arrivals, held, whole, out_sems)
+    query[...] = wide_dot(first_low[...], held[0]).astype(jnp.bfloat16)
+    key[...] = wide_dot(memory[...], held[1]).astype(jnp.bfloat16)
+    value[...] = wide_dot(memory[...], held[2]).astype(jnp.bfloat16)
+    attend_heads(query, key, value, allowed, context, logsum)
+    summed = RESIDUAL_SCALE * first[...] + wide_dot(context[...], held[3])
+    second[...], scaled[...], inverse[...] = norm_rows_of(summed, gains[2:3, :], gains[3:4, :])
+    second_low[...] = second[...].astype(jnp.bfloat16)
+    for copy in leaving:
+        copy.wait()
+
+
+def cross_forward(grid, place, first, first_low, memory, gains, ids_column, ids_row, pieces):
+    count, width = first.shape
+    others = memory.shape[0]
+    rows = pieces[0].shape[2]
+    low, full = jnp.bfloat16, jnp.float32
+    shape, other_shape = (count, width), (others, width)
+    return whole_call(
+        functools.partial(cross_forward_kernel, grid.depth, rows),
+        "cross_forward",
+        [(place, pltpu.SMEM), first, first_low, memory, gains, ids_column, ids_row]
+        + [(piece, pl.ANY) for piece in pieces],
+        [((4, width, width), low, pl.ANY), (shape, low), (other_shape, low), (other_shape, low), (shape, low)]
+        + [((count, 128), full), (shape, full), (shape, low), (shape, full), ((count, 1), full)],
+        [
+            pltpu.VMEM((4, width, width), low),
+            pltpu.VMEM((count, others), full),
+            pltpu.SemaphoreType.DMA((grid.count,)),
+            pltpu.SemaphoreType.DMA((grid.depth,)),
+        ],
+    )
+
+
+TANH_SCALE = 0.7978845608028654
+TANH_CUBE = 0.044715
+
+
+def expand_forward_kernel(depth, rows, place, second_low, *refs):
+    pieces, refs = refs[:6], refs[6:]
+    whole, active, slope, held, in_sems, out_sems = refs
+    arrivals = arrivals_of(depth, rows, place, pieces, held, in_sems)
+    leaving = pass_on(depth, rows, place, arrivals, held, whole, out_sems)
+    left = second_low[...]
+
+    def tile(j, carry):
+        lanes = pl.ds(pl.multiple_of(j * 512, 512), 512)
+        inner = wide_dot(left, held[:, lanes])
+        square = inner * inner
+        bend = jnp.tanh(TANH_SCALE * (inner * (1.0 + TANH_CUBE * square)))
+        half = 0.5 + 0.5 * bend
+        active[:, lanes] = (inner * half).astype(jnp.bfloat16)
+        slope[:, lanes] = half + (0.5 * TANH_SCALE) * inner * (1.0 - bend * bend) * (
+            1.0 + (3.0 * TANH_CUBE) * square
+        )
+        return carry
+
+    lax.fori_loop(0, held.shape[1] // 512, tile, 0)
+    for copy in leaving:
+        copy.wait()
+
+
+def expand_forward(grid, place, second_low, pieces):
+    count, width = second_low.shape
+    rows, hidden = pieces[0].shape[1:]
+    low = jnp.bfloat16
+    return whole_call(
+        functools.partial(expand_forward_kernel, grid.depth, rows),
+        "expand_forward",
+        [(place, pltpu.SMEM), second_low] + [(piece, pl.ANY) for piece in pieces],
+        [((width, hidden), low, pl.ANY), ((count, hidden), low), ((count, hidden), jnp.float32)],
+        [
+            pltpu.VMEM((width, hidden), low),
+            pltpu.SemaphoreType.DMA((grid.count,)),
+            pltpu.SemaphoreType.DMA((grid.depth,)),
+        ],
+    )
+
+
+def reduce_both_kernel(depth, rows, place, active, slope, second, gains, output_grad, *refs):
+    pieces, refs = refs[:6], refs[6:]
+    output, d_summed, d_branch, d_inner, norm_terms, held, in_sems = refs
+    arrivals = arrivals_of(depth, rows, place, pieces, held, in_sems)
+    for column in arrivals:
+        for copy in column:
+            copy.wait()
+    summed = RESIDUAL_SCALE * second[...] + wide_dot(active[...], held[...])
+    final, scaled, inverse = norm_rows_of(summed, gains[4:5, :], gains[5:6, :])
+    output[...] = final.astype(jnp.bfloat16)
+    d_sum, gain_term, shift_term = norm_rows_back(
+        output_grad[...].astype(jnp.float32), scaled, inverse, gains[4:5, :]
+    )
+    norm_terms[0:1, :] = gain_term
+    norm_terms[1:2, :] = shift_term
+    d_summed[...] = d_sum
+    d_branch[...] = d_sum.astype(jnp.bfloat16)
+    left = d_branch[...]
+
+    def tile(j, carry):
+        lanes = pl.ds(pl.multiple_of(j * 512, 512), 512)
+        d_active = dot_rows(left, held[lanes, :])
+        d_inner[:, lanes] = (d_active * slope[:, lanes]).astype(jnp.bfloat16)
+        return carry
+
+    lax.fori_loop(0, held.shape[0] // 512, tile, 0)
+
+
+def reduce_both(grid, place, active, slope, second, gains, output_grad, pieces):
+    count, width = second.shape
+    hidden = active.shape[1]
+    rows = pieces[0].shape[1]
+    low, full = jnp.bfloat16, jnp.float32
+    shape = (count, width)
+    return whole_call(
+        functools.partial(reduce_both_kernel, grid.depth, rows),
+        "reduce_both",
+        [(place, pltpu.SMEM), active, slope, second, gains, output_grad]
+        + [(piece, pl.ANY) for piece in pieces],
+        [(shape, low), (shape, full), (shape, low), ((count, hidden), low), ((2, width), full)],
+        [pltpu.VMEM((hidden, width), low), pltpu.SemaphoreType.DMA((grid.count,))],
+    )
+
+
+def expand_back_kernel(d_inner, expand, d_sum_three, scaled, inverse, gains, out_weight, d_summed, d_branch, d_context, norm_terms):
+    d_second = RESIDUAL_SCALE * d_sum_three[...] + dot_rows(d_inner[...], expand[...])
+    d_sum, norm_terms[0:1, :], norm_terms[1:2, :] = norm_rows_back(
+        d_second, scaled[...], inverse[...], gains[2:3, :]
+    )
+    d_summed[...] = d_sum
+    d_branch[...] = d_sum.astype(jnp.bfloat16)
+    d_context[...] = dot_rows(d_branch[...], out_weight[0]).astype(jnp.bfloat16)
+
+
+def expand_back(d_inner, expand, d_sum_three, scaled, inverse, gains, second_full):
+    shape = d_sum_three.shape
+    width = shape[1]
+    low, full = jnp.bfloat16, jnp.float32
+    return whole_call(
+        expand_back_kernel,
+        "expand_back",
+        [d_inner, expand, d_sum_three, scaled, inverse, gains, (second_full, (1, width, width), (3, 0, 0))],
+        [(shape, full), (shape, low), (shape, low), ((2, width), full)],
+    )
+
+
+def cross_back_kernel(
+    query, key, value, logsum, d_context, ids_column, ids_row, d_sum_two, scaled, inverse, gains,
+    query_weight, out_weight, d_query, d_key, d_value, d_summed, d_branch, d_context_one, norm_terms, allowed,
+):
+    cross_allowed(ids_column, ids_row, allowed)
+    attend_heads_back(query, key, value, allowed, logsum, d_context, d_query, d_key, d_value)
+    d_first = RESIDUAL_SCALE * d_sum_two[...] + dot_rows(d_query[...], query_weight[0])
+    d_sum, norm_terms[0:1, :], norm_terms[1:2, :] = norm_rows_back(
+        d_first, scaled[...], inverse[...], gains[0:1, :]
+    )
+    d_summed[...] = d_sum
+    d_branch[...] = d_sum.astype(jnp.bfloat16)
+    d_context_one[...] = dot_rows(d_branch[...], out_weight[0]).astype(jnp.bfloat16)
+
+
+def cross_back(query, key, value, logsum, d_context, ids_column, ids_row, d_sum_two, scaled, inverse, gains, second_full, first_full):
+    shape, other_shape = query.shape, key.shape
+    width = shape[1]
+    low, full = jnp.bfloat16, jnp.float32
+    block = (1, width, width)
+    return whole_call(
+        cross_back_kernel,
+        "cross_back",
+        [query, key, value, logsum, d_context, ids_column, ids_row, d_sum_two, scaled, inverse, gains]
+        + [(second_full, block, (0, 0, 0)), (first_full, block, (3, 0, 0))],
+        [(shape, low), (other_shape, low), (other_shape, low), (shape, full), (shape, low), (shape, low)]
+        + [((2, width), full)],
+        [pltpu.VMEM((shape[0], other_shape[0]), full)],
+    )
+
+
+def self_back_kernel(query, key, value, logsum, d_context, ids_column, ids_row, d_rows, allowed):
+    self_allowed(ids_column, ids_row, allowed)
+    count = query.shape[0]
+    outs = [d_rows.at[n * count : (n + 1) * count] for n in range(3)]
+    attend_heads_back(query, key, value, allowed, logsum, d_context, *outs)
+
+
+def self_back(query, key, value, logsum, d_context, ids_column, ids_row):
+    count, width = query.shape
+    return whole_call(
+        self_back_kernel,
+        "self_back",
+        [query, key, value, logsum, d_context, ids_column, ids_row],
+        [((3 * count, width), jnp.bfloat16)],
+        [pltpu.VMEM((count, count), jnp.float32)],
+    )[0]
+
+
+def inputs_back_kernel(d_rows, d_key, d_value, d_sum_one, w_query, w_key, w_value, w_key_two, w_value_two, tokens_grad, memory_grad):
+    count = d_sum_one.shape[0]
+    total = RESIDUAL_SCALE * d_sum_one[...]
+    for n, weight in enumerate((w_query, w_key, w_value)):
+        total += dot_rows(d_rows[n * count : (n + 1) * count, :], weight[0])
+    tokens_grad[...] = total
+    memory_grad[...] = dot_rows(d_key[...], w_key_two[0]) + dot_rows(d_value[...], w_value_two[0])
+
+
+def inputs_back(d_rows, d_key, d_value, d_sum_one, first_full, second_full):
+    width = d_key.shape[1]
+    block = (1, width, width)
+    return whole_call(
+        inputs_back_kernel,
+        "inputs_back",
+        [d_rows, d_key, d_value, d_sum_one]
+        + [(first_full, block, (n, 0, 0)) for n in range(3)]
+        + [(second_full, block, (n, 0, 0)) for n in (1, 2)],
+        [(d_sum_one.shape, jnp.float32), (d_key.shape, jnp.float32)],
+    )
+
+
+def turn(depth, rows, place, sources, turned):
+    z, c, y, x = place[0], place[1], place[2], place[3]
+    tokens = sources[0].shape[0]
+    for k in range(depth):
+        there = z ^ k
+        columns = pl.ds(pl.multiple_of((there * 2 + c) * (4 * rows), 4 * rows), 4 * rows)
+        for side, source in enumerate(sources):
+            block = source[:, columns].T
+            named = [block[n * rows : (n + 1) * rows] for n in range(4)]
+            named = [jnp.where(x == 0, named[n], named[n ^ 1]) for n in range(4)]
+            named = [jnp.where(y == 0, named[n], named[n ^ 2]) for n in range(4)]
+            for spot in range(4):
+                turned[spot, k * rows : (k + 1) * rows, side * tokens : (side + 1) * tokens] = named[spot]
+
+
+def spread(depth, rows, turned, rights, outs):
+    tokens = rights[0].shape[0]
+    own, over_x, over_y, low, high = outs
+    half = depth // 2
+    for spot in range(4):
+        part = turned[spot]
+        total = jnp.dot(part[:, :tokens], rights[0][...], preferred_element_type=jnp.float32)
+        total += jnp.dot(
+            part[:, tokens : 2 * tokens], rights[1][...], preferred_element_type=jnp.float32
+        )
+        total = total.astype(jnp.bfloat16).reshape(depth, rows, -1)
+        if spot < 3:
+            outs[spot][...] = total
+        else:
+            low[...] = total[:half]
+            high[...] = total[half:]
+
+
+def tiled_kernel(depth, rows, place, left, left_far, right, right_far, *refs):
+    outs, turned = refs[:5], refs[5]
+
+    @pl.when(pl.program_id(0) == 0)
+    def _():
+        turn(depth, rows, place, (left, left_far), turned)
+
+    spread(depth, rows, turned, (right, right_far), outs)
+
+
+def group_kernel(depth, rows, count, place, *refs):
+    inputs, outs, turned = refs[: 4 * count], refs[4 * count : 4 * count + 5], refs[-1]
+    for m in range(count):
+        left, left_far, right, right_far = inputs[4 * m : 4 * m + 4]
+        turn(depth, rows, place, (left, left_far), turned)
+        spread(depth, rows, turned, (right, right_far), [out.at[:, m] for out in outs])
+
+
+def piece_counts(grid):
+    return (grid.depth, grid.depth, grid.depth, grid.depth // 2, grid.depth // 2)
+
+
+def tiled_terms(grid, place, left, left_far, right, right_far, tile):
+    tokens, features = left.shape
+    width = right.shape[1]
+    rows = features // grid.count
+    left_row = 0
+    if left_far.shape[0] != tokens:
+        left_row = 4
+    return pl.pallas_call(
+        functools.partial(tiled_kernel, grid.depth, rows),
+        grid=(width // tile,),
+        out_shape=[jax.ShapeDtypeStruct((n, rows, width), jnp.bfloat16) for n in piece_counts(grid)],
+        in_specs=[
+            pl.BlockSpec(memory_space=pltpu.SMEM),
+            pl.BlockSpec((tokens, features), lambda j: (0, 0)),
+            pl.BlockSpec((tokens, features), lambda j: (left_row, 0)),
+        ]
+        + [pl.BlockSpec((tokens, tile), lambda j: (0, j))] * 2,
+        out_specs=[pl.BlockSpec((n, rows, tile), lambda j: (0, 0, j)) for n in piece_counts(grid)],
+        scratch_shapes=[pltpu.VMEM((4, grid.depth * rows, 2 * tokens), jnp.bfloat16)],
+        compiler_params=pltpu.CompilerParams(vmem_limit_bytes=40 * 2**20),
+        cost_estimate=pl.CostEstimate(flops=1, bytes_accessed=1, transcendentals=0),
+        name="terms",
+    )(place, left, left_far, right, right_far)
+
+
+def group_terms(grid, place, pairs):
+    width = 1024
+    rows = width // grid.count
+    arrays, specs = [], []
+    for tokens, left, right in pairs:
+        for near, far, row in (left, right):
+            arrays += [near, far]
+            specs += [pl.BlockSpec((tokens, width), lambda i, row=row: (row, 0))] * 2
+    most = max(tokens for tokens, _, _ in pairs)
+    shapes = [(n, len(pairs), rows, width) for n in piece_counts(grid)]
+    return pl.pallas_call(
+        functools.partial(group_kernel, grid.depth, rows, len(pairs)),
+        grid=(1,),
+        out_shape=[jax.ShapeDtypeStruct(shape, jnp.bfloat16) for shape in shapes],
+        in_specs=[pl.BlockSpec(memory_space=pltpu.SMEM)] + specs,
+        out_specs=[pl.BlockSpec(shape, lambda i: (0, 0, 0, 0)) for shape in shapes],
+        scratch_shapes=[pltpu.VMEM((4, grid.depth * rows, 2 * most), jnp.bfloat16)],
+        compiler_params=pltpu.CompilerParams(vmem_limit_bytes=48 * 2**20),
+        cost_estimate=pl.CostEstimate(flops=1, bytes_accessed=1, transcendentals=0),
+        name="terms",
+    )(place, *arrays)
+
+
+def settle_corner(grid, pieces):
+    low, high = pieces[3:]
+    return grid.move(low, dy=1), grid.move(high, dx=1)
+
+
+def settle_sides(grid, pieces, corner):
+    half = grid.depth // 2
+    over_x = pieces[1].at[:half].add(corner[0])
+    over_y = pieces[2].at[half:].add(corner[1])
+    return (over_x, over_y), (grid.move(over_x, dx=1), grid.move(over_y, dy=1))
+
+
+def settle_pairs(grid, pieces, sides):
+    half = grid.depth // 2
+    near, distant = [
+        (
+            pieces[0][part].astype(jnp.float32)
+            + sides[0][part].astype(jnp.float32)
+            + sides[1][part].astype(jnp.float32)
+        ).astype(jnp.bfloat16)
+        for part in (slice(0, half), slice(half, None))
+    ]
+    return near, grid.move(distant, dz=2)
+
+
+def settle_pair(grid, near, got):
+    leaving = (near[1].astype(jnp.float32) + got[1].astype(jnp.float32)).astype(jnp.bfloat16)
+    return leaving, grid.move(leaving, dz=1)
+
+
+def settle_total(near, got, last):
+    return near[0].astype(jnp.float32) + got[0].astype(jnp.float32) + last.astype(jnp.float32)
+
+
+def sum_norms(grid, terms_of):
+    held = terms_of.shape[1] // grid.count
+    total = jnp.pad(terms_of, ((0, 8 - terms_of.shape[0]), (0, 0)))
+    if not grid.fast:
+        total = lax.psum(total, ALL)
+    else:
+        for step in (dict(dc=1), dict(dy=1), dict(dx=1), dict(dz=1), dict(dz=2)):
+            total = total + grid.move(total, **step)
+    return lax.dynamic_slice(total, (0, lax.axis_index(ALL) * held), (8, held))
 
 
 def fetch(attention_rows, expand_rows, reduce_rows, norm_rows):
@@ -123,7 +779,7 @@
     )
 
 
-def per_device(
+def plain_device(
     tokens,
     memory,
     target_segments,
@@ -288,9 +944,188 @@
     )
 
 
+def per_device(
+    grid,
+    tokens,
+    memory,
+    target_segments,
+    source_segments,
+    self_query,
+    self_key,
+    self_value,
+    self_output,
+    cross_query,
+    cross_key,
+    cross_value,
+    cross_output,
+    expand_weight,
+    reduce_weight,
+    self_gain,
+    self_shift,
+    cross_gain,
+    cross_shift,
+    final_gain,
+    final_shift,
+    output_grad,
+):
+    if not grid.fast:
+        return plain_device(
+            tokens,
+            memory,
+            target_segments,
+            source_segments,
+            self_query,
+            self_key,
+            self_value,
+            self_output,
+            cross_query,
+            cross_key,
+            cross_value,
+            cross_output,
+            expand_weight,
+            reduce_weight,
+            self_gain,
+            self_shift,
+            cross_gain,
+            cross_shift,
+            final_gain,
+            final_shift,
+            output_grad,
+        )
+    place = grid.place()
+    held_rows = self_gain.shape[0]
+    norm_rows = jnp.stack([self_gain, self_shift, cross_gain, cross_shift, final_gain, final_shift])
+    extra = jnp.zeros((16, held_rows * grid.count), jnp.bfloat16)
+    extra = lax.dynamic_update_slice(extra, norm_rows, (0, lax.axis_index(ALL) * held_rows))
+    extra = extra.reshape(4, 32, 128)
+    first_rows = jnp.concatenate([jnp.stack([self_query, self_key, self_value, self_output]), extra], axis=-1)
+    second_rows = jnp.stack([cross_query, cross_key, cross_value, cross_output])
+    target_column, target_row = target_segments.reshape(-1, 1), target_segments
+    source_row = source_segments
+
+    first_own = gather_direct(grid, first_rows)
+    second_pair = gather_pair(grid, second_rows)
+    first_own, second_pair, expand_rows = after((first_own, second_pair, expand_weight))
+    first_sides = gather_sides(grid, first_own)
+    second_own = gather_pairs(grid, second_pair)
+    expand_pair = gather_pair(grid, expand_rows)
+    first_sides, second_own, expand_pair, reduce_rows = after(
+        (first_sides, second_own, expand_pair, reduce_weight)
+    )
+    first_ends = gather_corner(grid, first_own, first_sides)
+    second_sides = gather_sides(grid, second_own)
+    expand_own = gather_pairs(grid, expand_pair)
+    first_corner = gather_last(grid, *first_ends[:2])
+    first_pieces = (first_own, *first_sides, first_ends[2], *first_corner)
+    second_sides, expand_own, reduce_rows, first_pieces = after(
+        (second_sides, expand_own, reduce_rows, first_pieces)
+    )
+    second_ends = gather_corner(grid, second_own, second_sides)
+    expand_sides = gather_sides(grid, expand_own)
+    reduce_pair = gather_pair(grid, reduce_rows)
+    first_out = self_forward(grid, place, tokens, target_column, target_row, first_pieces)
+    first_out, second_ends, reduce_pair = after((first_out, second_ends, reduce_pair))
+    first_full, gains, query_one, key_one, value_one, context_one, logsum_one = first_out[:7]
+    first, first_low, first_scaled, first_inverse = first_out[7:]
+    reduce_own = gather_pairs(grid, reduce_pair)
+    second_corner = gather_last(grid, *second_ends[:2])
+    second_pieces = (second_own, *second_sides, second_ends[2], *second_corner)
+    expand_sides, reduce_own, second_pieces = after((expand_sides, reduce_own, second_pieces))
+    expand_ends = gather_corner(grid, expand_own, expand_sides)
+    reduce_sides = gather_sides(grid, reduce_own)
+    second_out = cross_forward(
+        grid, place, first, first_low, memory, gains, target_column, source_row, second_pieces
+    )
+    second_out, expand_ends = after((second_out, expand_ends))
+    second_full, query_two, key_two, value_two, context_two, logsum_two = second_out[:6]
+    second, second_low, second_scaled, second_inverse = second_out[6:]
+    held = jnp.concatenate([tokens, context_one, first_low, context_two, second_low, memory])
+    held_far = grid.move(held, dc=1)
+    expand_corner = gather_last(grid, *expand_ends[:2])
+    expand_pieces = (expand_own, *expand_sides, expand_ends[2], *expand_corner)
+    reduce_sides, expand_pieces = after((reduce_sides, expand_pieces))
+    reduce_ends = gather_corner(grid, reduce_own, reduce_sides)
+    expand_full, active, slope = expand_forward(grid, place, second_low, expand_pieces)
+    active, reduce_ends, held_far = after((active, reduce_ends, held_far))
+    active_far = grid.move(active, dc=1)
+    reduce_corner = gather_last(grid, *reduce_ends[:2])
+    reduce_pieces = (reduce_own, *reduce_sides, reduce_ends[2], *reduce_corner)
+    output, d_sum_three, d_branch_three, d_inner, final_terms = reduce_both(
+        grid, place, active, slope, second, gains, output_grad, reduce_pieces
+    )
+    d_branch_three_far = grid.move(d_branch_three, dc=1)
+    d_inner_far = grid.move(d_inner, dc=1)
+    d_sum_two, d_branch_two, d_context_two, cross_terms_of_norm = expand_back(
+        d_inner, expand_full, d_sum_three, second_scaled, second_inverse, gains, second_full
+    )
+    reduce_terms = tiled_terms(
+        grid, place, active, active_far, after(d_branch_three, d_branch_two), d_branch_three_far, 512
+    )
+    reduce_corner = settle_corner(grid, reduce_terms)
+    expand_terms = tiled_terms(
+        grid, place, second_low, held_far, after(d_inner, *reduce_terms), d_inner_far, 1024
+    )
+    expand_corner = settle_corner(grid, expand_terms)
+    reduce_mine, reduce_sides = settle_sides(grid, after(reduce_terms, *expand_terms), reduce_corner)
+    cross_out = cross_back(
+        query_two, key_two, value_two, logsum_two, after(d_context_two, *reduce_mine), target_column,
+        source_row, d_sum_two, first_scaled, first_inverse, gains, second_full, first_full,
+    )
+    d_query_two, d_key_two, d_value_two, d_sum_one, d_branch_one, d_context_one, self_terms_of_norm = cross_out
+    back = jnp.concatenate([d_branch_two, d_query_two, d_branch_one, d_key_two, d_value_two])
+    back_far = grid.move(back, dc=1)
+    expand_mine, expand_sides = settle_sides(grid, after(expand_terms, back), expand_corner)
+    norm_owned = sum_norms(grid, jnp.concatenate([self_terms_of_norm, cross_terms_of_norm, final_terms]))
+    back = after(back, *expand_mine)
+    pairs = [
+        (256, (held, held_far, 1), (back, back_far, 2)),
+        (256, (held, held_far, 2), (back, back_far, 1)),
+        (128, (held, held_far, 10), (back, back_far, 6)),
+        (128, (held, held_far, 10), (back, back_far, 7)),
+        (256, (held, held_far, 3), (back, back_far, 0)),
+    ]
+    cross_terms = group_terms(grid, place, pairs)
+    cross_corner = settle_corner(grid, cross_terms)
+    back_one = self_back(
+        query_one, key_one, value_one, logsum_one, after(d_context_one, *cross_terms), target_column, target_row
+    )
+    back_one_far = grid.move(back_one, dc=1)
+    reduce_near, reduce_got = settle_pairs(grid, after(reduce_terms, back_one), reduce_sides)
+    cross_mine, cross_sides = settle_sides(grid, after(cross_terms, reduce_near), cross_corner)
+    tokens_grad, memory_grad = inputs_back(
+        after(back_one, *cross_mine), d_key_two, d_value_two, d_sum_one, first_full, second_full
+    )
+    expand_near, expand_got = settle_pairs(grid, after(expand_terms, tokens_grad), expand_sides)
+    reduce_leaving, reduce_last = settle_pair(grid, after(reduce_near, expand_near), reduce_got)
+    back_one = after(back_one, reduce_leaving)
+    pairs = [(256, (held, held_far, 0), (back_one, back_one_far, i)) for i in range(3)]
+    self_terms = group_terms(grid, place, pairs)
+    self_corner = settle_corner(grid, self_terms)
+    expand_leaving, expand_last = settle_pair(grid, after(expand_near, *self_terms), expand_got)
+    cross_near, cross_got = settle_pairs(grid, after(cross_terms, expand_leaving), cross_sides)
+    self_mine, self_sides = settle_sides(grid, after(self_terms, cross_near), self_corner)
+    cross_leaving, cross_last = settle_pair(grid, after(cross_near, *self_mine), cross_got)
+    self_near, self_got = settle_pairs(grid, after(self_terms, cross_leaving), self_sides)
+    self_leaving, self_last = settle_pair(grid, self_near, self_got)
+    reduce_term = settle_total(reduce_near, reduce_got, reduce_last)
+    expand_term = settle_total(expand_near, expand_got, expand_last)
+    cross_owned = settle_total(cross_near, cross_got, cross_last)
+    self_owned = settle_total(self_near, self_got, self_last)
+    return (
+        output,
+        tokens_grad,
+        memory_grad,
+        *[self_owned[i] for i in range(3)],
+        *[cross_owned[i] for i in range(5)],
+        expand_term,
+        reduce_term,
+        *[norm_owned[i] for i in range(6)],
+    )
+
+
 def solution(mesh):
     return jax.shard_map(
-        per_device,
+        functools.partial(per_device, Grid(mesh)),
         mesh=mesh,
         in_specs=(
             P(("dp", "fsdp"), None),

time: 1920 us -> 498 us (0.26)
  waiting for transfers between devices: 1620 us -> 242 us
  matrix products: 134 us -> 0 us
  Pallas kernels: 0 us -> 125 us
  blocking collectives: 71.5 us -> 0 us
  starting transfers between devices: 0.67 us -> 61.2 us
  local copies, waits for them, and re-layouts: 67.2 us -> 23.8 us
  other arithmetic: 6.86 us -> 34.2 us
    reduce_scatter x3 -> x0, waiting for transfers between devices: 1410 us -> none  [the longest x1 702 us: settle(): lax.psum_scatter(attention_terms, ('dp', 'fsdp'), scatter_dimension=1, ti...]
    ppermute x0 -> x68, waiting for transfers between devices: none -> 242 us  [move(): lax.ppermute(value, ALL, [(index ^ offset, index) for index in range(self...]
    all_gather x3 -> x0, waiting for transfers between devices: 162 us -> none  [the longest x1 71 us: fetch(): lax.all_gather(reduce_rows, ('dp', 'fsdp'), axis=0, tiled=True)]
    dot_general x42 -> x0, matrix products: 134 us -> none  [the longest x10 42.5 us: across(): jnp.einsum('ti,tj->ij', left, right, preferred_element_type=jnp.float32)]
    pallas_call x0 -> x12, Pallas kernels: none -> 125 us  [the longest x8 104 us: whole_call(): pl.pallas_call(body, grid=(1,), out_shape=outs, in_specs=specs, out_specs...]
    all_gather x1 -> x0, blocking collectives: 71.5 us -> none  [fetch(): lax.all_gather(norm_rows, ('dp', 'fsdp'), axis=1, tiled=True)]
    ppermute x0 -> x68, starting transfers between devices: none -> 61.2 us  [move(): lax.ppermute(value, ALL, [(index ^ offset, index) for index in range(self...]
    unnamed x8 -> x0, waiting for transfers between devices: 42 us -> none
  transfers between devices with their start and end apart: 7 -> 68, of which waited for: 7 -> 26; matrix products, arithmetic and copies ran while one was open for 7% -> 9% of each run, Pallas kernels for 0% -> 26%
where the time goes in v2:
time: 498 us; the launch traced here: 489 us
  waiting for transfers between devices  242 us (49%)
  Pallas kernels  125 us (25%)
  starting transfers between devices  61.2 us (12%)
  other arithmetic  34.2 us (7%)
  local copies, waits for them, and re-layouts  23.8 us (5%)
    ppermute x68, waiting for transfers between devices, move(): lax.ppermute(value, ALL, [(index ^ offset, index) for index in range(self...  242 us
    pallas_call x8, Pallas kernels, whole_call(): pl.pallas_call(body, grid=(1,), out_shape=outs, in_specs=specs, out_specs...  104 us
    ppermute x68, starting transfers between devices, move(): lax.ppermute(value, ALL, [(index ^ offset, index) for index in range(self...  61.2 us
    unnamed x131, local copies, waits for them, and re-layouts  15.1 us
    pallas_call x2, Pallas kernels, group_terms(): pl.pallas_call(functools.partial(group_kernel, grid.depth, rows, len(pair...  11 us
    pallas_call x2, Pallas kernels, tiled_terms(): pl.pallas_call(functools.partial(tiled_kernel, grid.depth, rows), grid=(w...  10.2 us
  transfers between devices with their start and end apart: 68, of which 26 were waited for; matrix products, arithmetic and copies ran while one was open for 9% of the time, Pallas kernels for 26%

profile of v2, /device:TPU:0, one launch (start us, length us, event | category | flops | bytes accessed | tf_op | source)
XLA Modules:
  0.0 489.0 jit_solution(10927618128051926722)
XLA Ops:
  12.3 8.5 %collective-permute-done.2 = bf16[4,32,1152]{2,1,0:T(8,128)(2,1)S(1)} collective-permute-done((bf16[4,32,1152]{2,1,0:T(8,128)(2,1)S(1)}, bf16[4,32,1152]{2,1,0:T(8,128)(2,1)S(1)}, u32[]{:S(2)}, u32[]{:S(2)}) %collective-permute-start.2) | collective-permute-done | bytes 294944 | tf_op jit(solution)/shard_map/ppermute | solution.py:32
  20.8 14.4 %collective-permute-done.1 = bf16[4,32,1152]{2,1,0:T(8,128)(2,1)S(1)} collective-permute-done((bf16[4,32,1152]{2,1,0:T(8,128)(2,1)S(1)}, bf16[4,32,1152]{2,1,0:T(8,128)(2,1)S(1)}, u32[]{:S(2)}, u32[]{:S(2)}) %collective-permute-start.1) | collective-permute-done | bytes 294944 | tf_op jit(solution)/shard_map/ppermute | solution.py:32
  41.9 8.8 %collective-permute-done.7 = bf16[32,4096]{1,0:T(8,128)(2,1)S(1)} collective-permute-done((bf16[32,4096]{1,0:T(8,128)(2,1)S(1)}, bf16[32,4096]{1,0:T(8,128)(2,1)S(1)}, u32[]{:S(2)}, u32[]{:S(2)}) %collective-permute-start.7) | collective-permute-done | bytes 262176 | tf_op jit(solution)/shard_map/ppermute | solution.py:32
  50.7 12.6 %collective-permute-done.6 = bf16[2,4,32,1024]{3,2,1,0:T(8,128)(2,1)S(1)} collective-permute-done((bf16[2,4,32,1024]{3,2,1,0:T(8,128)(2,1)S(1)}, bf16[2,4,32,1024]{3,2,1,0:T(8,128)(2,1)S(1)}, u32[]{:S(2)}, u32[]{:S(2)}) %collective-permute-start.6) | collective-permute-done | bytes 524320 | tf_op jit(solution)/shard_map/ppermute | solution.py:32
  66.8 13.4 %collective-permute-done.12 = bf16[2,4,32,1152]{3,2,1,0:T(8,128)(2,1)S(1)} collective-permute-done((bf16[2,4,32,1152]{3,2,1,0:T(8,128)(2,1)S(1)}, bf16[2,4,32,1152]{3,2,1,0:T(8,128)(2,1)S(1)}, u32[]{:S(2)}, u32[]{:S(2)}) %collective-permute-start.12) | collective-permute-done | bytes 589856 | tf_op jit(solution)/shard_map/ppermute | solution.py:32
  82.6 25.8 %collective-permute-done.10 = bf16[2,32,4096]{2,1,0:T(8,128)(2,1)S(1)} collective-permute-done((bf16[2,32,4096]{2,1,0:T(8,128)(2,1)S(1)}, bf16[2,32,4096]{2,1,0:T(8,128)(2,1)S(1)}, u32[]{:S(2)}, u32[]{:S(2)}) %collective-permute-start.10) | collective-permute-done | bytes 524320 | tf_op jit(solution)/shard_map/ppermute | solution.py:32
  117.0 16.8 %self_forward.1 = (bf16[4,1024,1024]{2,1,0:T(8,128)(2,1)}, f32[8,1024]{1,0:T(8,128)}, bf16[256,1024]{1,0:T(8,128)(2,1)}, bf16[256,1024]{1,0:T(8,128)(2,1)}, bf16...) custom-call(s32[4]{0:T(128)} %pad_add_fusion.place, ...), custom_call_target="tpu_custom_call" | custom-call | flops 1 | bytes 1 | tf_op jit(solution)/shard_map/self_forward/pallas_call | solution.py:97
  136.7 24.3 %collective-permute-done.21 = bf16[2,128,1024]{2,1,0:T(8,128)(2,1)S(1)} collective-permute-done((bf16[2,128,1024]{2,1,0:T(8,128)(2,1)S(1)}, bf16[2,128,1024]{2,1,0:T(8,128)(2,1)S(1)}, u32[]{:S(2)}, u32[]{:S(2)}) %collective-permute-start.21) | collective-permute-done | bytes 524320 | tf_op jit(solution)/shard_map/ppermute | solution.py:32
  169.8 16.4 %cross_forward.1 = (bf16[4,1024,1024]{2,1,0:T(8,128)(2,1)}, bf16[256,1024]{1,0:T(8,128)(2,1)}, bf16[128,1024]{1,0:T(8,128)(2,1)}, bf16[128,1024]{1,0:T(8,128)(2,...) custom-call(s32[4]{0:T(128)} %pad_add_fusion.place, ...), custom_call_target="tpu_custom_call" | custom-call | flops 1 | bytes 1 | tf_op jit(solution)/shard_map/cross_forward/pallas_call | solution.py:97
  189.0 15.2 %collective-permute-done.26.refs_1_ = bf16[4,128,1024]{2,1,0:T(8,128)(2,1)S(1)} collective-permute-done((bf16[4,128,1024]{2,1,0:T(8,128)(2,1)S(1)}, bf16[4,128,1024]{2,1,0:T(8,128)(2,1)S(1)}, u32[]{:S(2)}, u32[]{:S(2)}) %collective-permute-start.26) | collective-permute-done | bytes 1048608 | tf_op jit(solution)/shard_map/ppermute | solution.py:32
  209.7 15.5 %expand_forward.1 = (bf16[1024,4096]{1,0:T(8,128)(2,1)}, bf16[256,4096]{1,0:T(8,128)(2,1)}, f32[256,4096]{1,0:T(8,128)}) custom-call(s32[4]{0:T(128)} %pad_add_fusion.place, bf16[256,1024]{1,0:T(8,128)(2,1)} %get-tuple-element.321.second_low.left, bf16[4,32,4096]{2,1,0:T(8,128)(2,1)} %copy-done.18, bf16[4,32,4096]{2,1,0:T(8,128)(2,1)} %copy-done.23, ...), custom_call_target="tpu_custom_call" | custom-call | flops 1 | bytes 1 | tf_op jit(solution)/shard_map/expand_forward/pallas_call | solution.py:97
  229.1 15.4 %reduce_both.1 = (bf16[256,1024]{1,0:T(8,128)(2,1)}, f32[256,1024]{1,0:T(8,128)}, bf16[256,1024]{1,0:T(8,128)(2,1)}, bf16[256,4096]{1,0:T(8,128)(2,1)}, f32[2,1024]{1,0:T(2,128)}) custom-call(s32[4]{0:T(128)} %pad_add_fusion.place, bf16[256,4096]{1,0:T(8,128)(2,1)} %get-tuple-element.337.active.left, f32[256,4096]{1,0:T(8,128)} %get-tuple-element.338.slope, ...), custom_call_target="tpu_custom_call" | custom-call | flops 1 | bytes 1 | tf_op jit(solution)/shard_map/reduce_both/pallas_call | solution.py:97
  245.1 9.5 %expand_back.1 = (f32[256,1024]{1,0:T(8,128)}, bf16[256,1024]{1,0:T(8,128)(2,1)}, bf16[256,1024]{1,0:T(8,128)(2,1)}, f32[2,1024]{1,0:T(2,128)}) custom-call(bf16[256,4096]{1,0:T(8,128)(2,1)} %get-tuple-element.368.d_inner.right, bf16[1024,4096]{1,0:T(8,128)(2,1)} %get-tuple-element.353.expand, f32[256,1024]{1,0:T(8,128)} %get-tuple-element.354.d_sum_three, ...), custom_call_target="tpu_custom_call" | custom-call | flops 1 | bytes 1 | tf_op jit(solution)/shard_map/expand_back/pallas_call | solution.py:97
  254.6 5.3 %terms.4 = (bf16[4,128,1024]{2,1,0:T(8,128)(2,1)S(1)}, bf16[4,128,1024]{2,1,0:T(8,128)(2,1)S(1)}, bf16[4,128,1024]{2,1,0:T(8,128)(2,1)S(1)}, bf16[2,128,1024]{2,1,0:T(8,128)(2,1)S(1)}, bf16[2,128,1024]{2,1,0:T(8,128)(2,1)S(1)}) custom-call(s32[4]{0:T(128)S(1)} %copy-done.9, bf16[256,4096]{1,0:T(8,128)(2,1)} %get-tuple-element.337.active.left, ...), custom_call_target="tpu_custom_call" | custom-call | flops 1 | bytes 1 | tf_op jit(solution)/shard_map/terms/pallas_call | solution.py:585
  278.9 11.4 %cross_back.1 = (bf16[256,1024]{1,0:T(8,128)(2,1)}, bf16[128,1024]{1,0:T(8,128)(2,1)}, bf16[128,1024]{1,0:T(8,128)(2,1)}, f32[256,1024]{1,0:T(8,128)}, bf16[256,...) custom-call(bf16[256,1024]{1,0:T(8,128)(2,1)} %get-tuple-element.348.query, ...), custom_call_target="tpu_custom_call" | custom-call | flops 1 | bytes 1 | tf_op jit(solution)/shard_map/cross_back/pallas_call | solution.py:97
  300.5 7.0 %collective-permute-done.40 = bf16[2,32,4096]{2,1,0:T(8,128)(2,1)S(1)} collective-permute-done((bf16[2,32,4096]{2,1,0:T(8,128)(2,1)S(1)}, bf16[2,32,4096]{2,1,0:T(8,128)(2,1)S(1)}, u32[]{:S(2)}, u32[]{:S(2)}) %collective-permute-start.40) | collective-permute-done | bytes 524320 | tf_op jit(solution)/shard_map/ppermute | solution.py:32
  310.9 6.6 %terms.6 = (bf16[4,5,32,1024]{3,2,1,0:T(8,128)(2,1)S(1)}, bf16[4,5,32,1024]{3,2,1,0:T(8,128)(2,1)S(1)}, bf16[4,5,32,1024]{3,2,1,0:T(8,128)(2,1)S(1)}, bf16[2,5,3...) custom-call(s32[4]{0:T(128)S(1)} %copy-done.9, bf16[1408,1024]{1,0:T(8,128)(2,1)} %copy-done.12, ...), custom_call_target="tpu_custom_call" | custom-call | flops 1 | bytes 1 | tf_op jit(solution)/shard_map/terms/pallas_call | solution.py:613
  321.7 10.3 %self_back.1.d_rows.refs_2_.refs_6_.refs_10_ = bf16[768,1024]{1,0:T(8,128)(2,1)} custom-call(bf16[256,1024]{1,0:T(8,128)(2,1)} %get-tuple-element.344.query, bf16[256,1024]{1,0:T(8,128)(2,1)} %get-tuple-element.345.key, bf16[256,1024]{1,0:T(8,128)(2,1)} %get-tuple-element.346.value, f32[256,128]{1,0:T(8,128)} %get-tuple-element.347.logsum, ...), custom_call_target="tpu_custom_call" | custom-call | flops 1 | bytes 1 | tf_op jit(solution)/shard_map/self_back/pallas_call | solution.py:97
  338.9 27.3 %collective-permute-done.45 = bf16[2,5,32,1024]{3,2,1,0:T(8,128)(2,1)} collective-permute-done((bf16[2,5,32,1024]{3,2,1,0:T(8,128)(2,1)S(1)}, bf16[2,5,32,1024]{3,2,1,0:T(8,128)(2,1)}, u32[]{:S(2)}, u32[]{:S(2)}) %collective-permute-start.45) | collective-permute-done | bytes 655392 | tf_op jit(solution)/shard_map/ppermute | solution.py:32
  368.5 8.9 %inputs_back.1 = (f32[256,1024]{1,0:T(8,128)}, f32[128,1024]{1,0:T(8,128)}) custom-call(bf16[768,1024]{1,0:T(8,128)(2,1)} %self_back.1.d_rows.refs_2_.refs_6_.refs_10_, bf16[128,1024]{1,0:T(8,128)(2,1)} %get-tuple-element.384.d_key, bf16[128,1024]{1,0:T(8,128)(2,1)} %get-tuple-element.385.d_value, f32[256,1024]{1,0:T(8,128)} %get-tuple-element.399.d_sum_one, ...), custom_call_target="tpu_custom_call" | custom-call | flops 1 | bytes 1 | tf_op jit(solution)/shard_map/inputs_back/pallas_call | solution.py:97
  395.1 7.4 %collective-permute-done.48 = bf16[2,128,1024]{2,1,0:T(8,128)(2,1)} collective-permute-done((bf16[2,128,1024]{2,1,0:T(8,128)(2,1)}, bf16[2,128,1024]{2,1,0:T(8,128)(2,1)}, u32[]{:S(2)}, u32[]{:S(2)}) %collective-permute-start.48) | collective-permute-done | bytes 524320 | tf_op jit(solution)/shard_map/ppermute | solution.py:32
  421.3 5.2 %collective-permute-done.51 = bf16[4,5,32,1024]{3,2,1,0:T(8,128)(2,1)S(1)} collective-permute-done((bf16[4,5,32,1024]{3,2,1,0:T(8,128)(2,1)S(1)}, bf16[4,5,32,1024]{3,2,1,0:T(8,128)(2,1)S(1)}, u32[]{:S(2)}, u32[]{:S(2)}) %collective-permute-start.51) | collective-permute-done | bytes 1310752 | tf_op jit(solution)/shard_map/ppermute | solution.py:32
  439.6 23.0 %collective-permute-done.55 = bf16[2,5,32,1024]{3,2,1,0:T(8,128)(2,1)S(1)} collective-permute-done((bf16[2,5,32,1024]{3,2,1,0:T(8,128)(2,1)S(1)}, bf16[2,5,32,1024]{3,2,1,0:T(8,128)(2,1)S(1)}, u32[]{:S(2)}, u32[]{:S(2)}) %collective-permute-start.55) | collective-permute-done | bytes 655392 | tf_op jit(solution)/shard_map/ppermute | solution.py:32
  466.8 10.0 %collective-permute-done.60 = bf16[5,32,1024]{2,1,0:T(8,128)(2,1)S(1)} collective-permute-done((bf16[5,32,1024]{2,1,0:T(8,128)(2,1)S(1)}, bf16[5,32,1024]{2,1,0:T(8,128)(2,1)S(1)}, u32[]{:S(2)}, u32[]{:S(2)}) %collective-permute-start.60) | collective-permute-done | bytes 327712 | tf_op jit(solution)/shard_map/ppermute | solution.py:32
  (318 shorter events, 167.9 us)
Async XLA Ops:
  35.4 28.1 %collective-permute-start.4 = (bf16[4,4,32,1152]{3,2,1,0:T(8,128)(2,1)S(1)}, bf16[4,4,32,1152]{3,2,1,0:T(8,128)(2,1)S(1)}, u32[]{:S(2)}, u32[]{:S(2)}) collective-permute-start(bf16[4,4,32,1152]{3,2,1,0:T(8,128)(2,1)S(1)} %pad_maximum_fusion.4.refs_0_), channel_id=1, source_target_pairs={{1,0},{0,1},{3,2},{2,3},{5,4},{4,5},{7,6},{6,7},{9,8},{8,9},{11,10... | collective-permute-start | bytes 3538952 | tf_op jit(solution)/shard_map/ppermute | solution.py:32
  64.3 44.4 %collective-permute-start.11 = (bf16[12,4,32,1152]{3,2,1,0:T(8,128)(2,1)S(1)}, bf16[12,4,32,1152]{3,2,1,0:T(8,128)(2,1)}, u32[]{:S(2)}, u32[]{:S(2)}) collective-permute-start(bf16[12,4,32,1152]{3,2,1,0:T(8,128)(2,1)S(1)} %pad_maximum_fusion), channel_id=1, source_target_pairs={{4,0},{5,1},{6,2},{7,3},{0,4},{1,5},{2,6},{3,7},{12,8},{13,9},{14,... | collective-permute-start | bytes 10616840 | tf_op jit(solution)/shard_map/ppermute | solution.py:32
  81.6 27.0 %collective-permute-start.14 = (bf16[4,4,32,1152]{3,2,1,0:T(8,128)(2,1)S(1)}, bf16[4,4,32,1152]{3,2,1,0:T(8,128)(2,1)S(1)}, u32[]{:S(2)}, u32[]{:S(2)}) collective-permute-start(bf16[4,4,32,1152]{3,2,1,0:T(8,128)(2,1)S(1)} %constant_dynamic-update-slice_fusion.refs_4_), channel_id=1, source_target_pairs={{4,0},{5,1},{6,2},{7,3},{0,4},{1,5},{2,6},{3,7},{12,8},{13,9},{14,... | collective-permute-start | bytes 3538952 | tf_op jit(solution)/shard_map/ppermute | solution.py:32
  81.7 26.9 %collective-permute-start.8 = (bf16[4,4,32,1024]{3,2,1,0:T(8,128)(2,1)S(1)}, bf16[4,4,32,1024]{3,2,1,0:T(8,128)(2,1)S(1)}, u32[]{:S(2)}, u32[]{:S(2)}) collective-permute-start(bf16[4,4,32,1024]{3,2,1,0:T(8,128)(2,1)S(1)} %pad_maximum_fusion.5.refs_0_), channel_id=1, source_target_pairs={{1,0},{0,1},{3,2},{2,3},{5,4},{4,5},{7,6},{6,7},{9,8},{8,9},{11,10... | collective-permute-start | bytes 3145736 | tf_op jit(solution)/shard_map/ppermute | solution.py:32
  116.5 44.6 %collective-permute-start.19 = (bf16[4,32,4096]{2,1,0:T(8,128)(2,1)S(1)}, bf16[4,32,4096]{2,1,0:T(8,128)(2,1)S(1)}, u32[]{:S(2)}, u32[]{:S(2)}) collective-permute-start(bf16[4,32,4096]{2,1,0:T(8,128)(2,1)S(1)} %pad_maximum_fusion.6.refs_0_), channel_id=1, source_target_pairs={{1,0},{0,1},{3,2},{2,3},{5,4},{4,5},{7,6},{6,7},{9,8},{8,9},{11,10... | collective-permute-start | bytes 3145736 | tf_op jit(solution)/shard_map/ppermute | solution.py:32
  133.8 27.3 %collective-permute-start.20 = (bf16[4,32,4096]{2,1,0:T(8,128)(2,1)S(1)}, bf16[4,32,4096]{2,1,0:T(8,128)(2,1)S(1)}, u32[]{:S(2)}, u32[]{:S(2)}) collective-permute-start(bf16[4,32,4096]{2,1,0:T(8,128)(2,1)S(1)} %pad_maximum_fusion.6.refs_0_), channel_id=1, source_target_pairs={{2,0},{3,1},{0,2},{1,3},{6,4},{7,5},{4,6},{5,7},{10,8},{11,9},{8,1... | collective-permute-start | bytes 3145736 | tf_op jit(solution)/shard_map/ppermute | solution.py:32
  169.0 35.2 %collective-permute-start.26 = (bf16[4,128,1024]{2,1,0:T(8,128)(2,1)S(1)}, bf16[4,128,1024]{2,1,0:T(8,128)(2,1)S(1)}, u32[]{:S(2)}, u32[]{:S(2)}) collective-permute-start(bf16[4,128,1024]{2,1,0:T(8,128)(2,1)S(1)} %pad_maximum_fusion.7.refs_0_), channel_id=1, source_target_pairs={{1,0},{0,1},{3,2},{2,3},{5,4},{4,5},{7,6},{6,7},{9,8},{8,9},{11,10... | collective-permute-start | bytes 3145736 | tf_op jit(solution)/shard_map/ppermute | solution.py:32
  169.5 34.7 %collective-permute-start.27 = (bf16[4,128,1024]{2,1,0:T(8,128)(2,1)S(1)}, bf16[4,128,1024]{2,1,0:T(8,128)(2,1)S(1)}, u32[]{:S(2)}, u32[]{:S(2)}) collective-permute-start(bf16[4,128,1024]{2,1,0:T(8,128)(2,1)S(1)} %pad_maximum_fusion.7.refs_0_), channel_id=1, source_target_pairs={{2,0},{3,1},{0,2},{1,3},{6,4},{7,5},{4,6},{5,7},{10,8},{11,9},{8,1... | collective-permute-start | bytes 3145736 | tf_op jit(solution)/shard_map/ppermute | solution.py:32
  225.7 28.9 %collective-permute-start.34 = (bf16[256,4096]{1,0:T(8,128)(2,1)}, bf16[256,4096]{1,0:T(8,128)(2,1)S(1)}, u32[]{:S(2)}, u32[]{:S(2)}) collective-permute-start(bf16[256,4096]{1,0:T(8,128)(2,1)} %get-tuple-element.337.active.left), channel_id=1, source_target_pairs={{4,0},{5,1},{6,2},{7,3},{0,4},{1,5},{2,6},{3,7},{12,8},{13,9},{14,... | collective-permute-start | bytes 6291464 | tf_op jit(solution)/shard_map/ppermute | solution.py:32
  267.8 30.6 %collective-permute-start.39 = (bf16[2,32,4096]{2,1,0:T(8,128)(2,1)}, bf16[2,32,4096]{2,1,0:T(8,128)(2,1)S(1)}, u32[]{:S(2)}, u32[]{:S(2)}) collective-permute-start(bf16[2,32,4096]{2,1,0:T(8,128)(2,1)} %get-tuple-element.372), channel_id=1, source_target_pairs={{2,0},{3,1},{0,2},{1,3},{6,4},{7,5},{4,6},{5,7},{10,8},{11,9},{8,1... | collective-permute-start | bytes 1572872 | tf_op jit(solution)/shard_map/ppermute | solution.py:32
  294.8 37.1 %collective-permute-start.42 = (bf16[4,128,1024]{2,1,0:T(8,128)(2,1)}, bf16[4,128,1024]{2,1,0:T(8,128)(2,1)}, u32[]{:S(2)}, u32[]{:S(2)}) collective-permute-start(bf16[4,128,1024]{2,1,0:T(8,128)(2,1)} %add_dynamic-update-slice_fusion.5), channel_id=1, source_target_pairs={{1,0},{0,1},{3,2},{2,3},{5,4},{4,5},{7,6},{6,7},{9,8},{8,9},{11,10... | collective-permute-start | bytes 3145736 | tf_op jit(solution)/shard_map/ppermute | solution.py:32
  319.1 58.3 %collective-permute-start.47 = (bf16[4,32,4096]{2,1,0:T(8,128)(2,1)}, bf16[4,32,4096]{2,1,0:T(8,128)(2,1)}, u32[]{:S(2)}, u32[]{:S(2)}) collective-permute-start(bf16[4,32,4096]{2,1,0:T(8,128)(2,1)} %add_dynamic-update-slice_fusion.2), channel_id=1, source_target_pairs={{2,0},{3,1},{0,2},{1,3},{6,4},{7,5},{4,6},{5,7},{10,8},{11,9},{8,1... | collective-permute-start | bytes 3145736 | tf_op jit(solution)/shard_map/ppermute | solution.py:32
  319.6 57.8 %collective-permute-start.46 = (bf16[4,32,4096]{2,1,0:T(8,128)(2,1)}, bf16[4,32,4096]{2,1,0:T(8,128)(2,1)}, u32[]{:S(2)}, u32[]{:S(2)}) collective-permute-start(bf16[4,32,4096]{2,1,0:T(8,128)(2,1)} %add_dynamic-update-slice_fusion.3), channel_id=1, source_target_pairs={{1,0},{0,1},{3,2},{2,3},{5,4},{4,5},{7,6},{6,7},{9,8},{8,9},{11,10... | collective-permute-start | bytes 3145736 | tf_op jit(solution)/shard_map/ppermute | solution.py:32
  320.0 46.2 %collective-permute-start.45 = (bf16[2,5,32,1024]{3,2,1,0:T(8,128)(2,1)S(1)}, bf16[2,5,32,1024]{3,2,1,0:T(8,128)(2,1)}, u32[]{:S(2)}, u32[]{:S(2)}) collective-permute-start(bf16[2,5,32,1024]{3,2,1,0:T(8,128)(2,1)S(1)} %get-tuple-element.393), channel_id=1, source_target_pairs={{1,0},{0,1},{3,2},{2,3},{5,4},{4,5},{7,6},{6,7},{9,8},{8,9},{11,10... | collective-permute-start | bytes 1966088 | tf_op jit(solution)/shard_map/ppermute | solution.py:32
  332.0 50.7 %collective-permute-start.63 = (f32[8,1024]{1,0:T(8,128)S(1)}, f32[8,1024]{1,0:T(8,128)S(1)}, u32[]{:S(2)}, u32[]{:S(2)}) collective-permute-start(f32[8,1024]{1,0:T(8,128)S(1)} %select_maximum_fusion), channel_id=1, source_target_pairs={{4,0},{5,1},{6,2},{7,3},{0,4},{1,5},{2,6},{3,7},{12,8},{13,9},{14,... | collective-permute-start | bytes 98312 | tf_op jit(solution)/shard_map/ppermute | solution.py:32
  337.0 67.2 %collective-permute-start.49 = (bf16[768,1024]{1,0:T(8,128)(2,1)S(1)}, bf16[768,1024]{1,0:T(8,128)(2,1)S(1)}, u32[]{:S(2)}, u32[]{:S(2)}) collective-permute-start(bf16[768,1024]{1,0:T(8,128)(2,1)S(1)} %copy-done.1), channel_id=1, source_target_pairs={{4,0},{5,1},{6,2},{7,3},{0,4},{1,5},{2,6},{3,7},{12,8},{13,9},{14,... | collective-permute-start | bytes 4718600 | tf_op jit(solution)/shard_map/ppermute | solution.py:32
  366.2 36.3 %collective-permute-start.48 = (bf16[2,128,1024]{2,1,0:T(8,128)(2,1)}, bf16[2,128,1024]{2,1,0:T(8,128)(2,1)}, u32[]{:S(2)}, u32[]{:S(2)}) collective-permute-start(bf16[2,128,1024]{2,1,0:T(8,128)(2,1)} %get-tuple-element.423), channel_id=1, source_target_pairs={{16,0},{17,1},{18,2},{19,3},{20,4},{21,5},{22,6},{23,7},{24,8},{25... | collective-permute-start | bytes 1572872 | tf_op jit(solution)/shard_map/ppermute | solution.py:32
  379.7 34.7 %collective-permute-start.50 = (bf16[2,32,4096]{2,1,0:T(8,128)(2,1)S(1)}, bf16[2,32,4096]{2,1,0:T(8,128)(2,1)S(1)}, u32[]{:S(2)}, u32[]{:S(2)}) collective-permute-start(bf16[2,32,4096]{2,1,0:T(8,128)(2,1)S(1)} %get-tuple-element.421), channel_id=1, source_target_pairs={{16,0},{17,1},{18,2},{19,3},{20,4},{21,5},{22,6},{23,7},{24,8},{25... | collective-permute-start | bytes 1572872 | tf_op jit(solution)/shard_map/ppermute | solution.py:32
  390.6 29.2 %collective-permute-start.52 = (bf16[4,5,32,1024]{3,2,1,0:T(8,128)(2,1)}, bf16[4,5,32,1024]{3,2,1,0:T(8,128)(2,1)S(1)}, u32[]{:S(2)}, u32[]{:S(2)}) collective-permute-start(bf16[4,5,32,1024]{3,2,1,0:T(8,128)(2,1)} %add_dynamic-update-slice_fusion), channel_id=1, source_target_pairs={{2,0},{3,1},{0,2},{1,3},{6,4},{7,5},{4,6},{5,7},{10,8},{11,9},{8,1... | collective-permute-start | bytes 3932168 | tf_op jit(solution)/shard_map/ppermute | solution.py:32
  394.8 31.7 %collective-permute-start.51 = (bf16[4,5,32,1024]{3,2,1,0:T(8,128)(2,1)S(1)}, bf16[4,5,32,1024]{3,2,1,0:T(8,128)(2,1)S(1)}, u32[]{:S(2)}, u32[]{:S(2)}) collective-permute-start(bf16[4,5,32,1024]{3,2,1,0:T(8,128)(2,1)S(1)} %copy-done.32), channel_id=1, source_target_pairs={{1,0},{0,1},{3,2},{2,3},{5,4},{4,5},{7,6},{6,7},{9,8},{8,9},{11,10... | collective-permute-start | bytes 3932168 | tf_op jit(solution)/shard_map/ppermute | solution.py:32
  402.5 34.6 %collective-permute-start.67 = (f32[8,1024]{1,0:T(8,128)S(1)}, f32[8,1024]{1,0:T(8,128)S(1)}, u32[]{:S(2)}, u32[]{:S(2)}) collective-permute-start(f32[8,1024]{1,0:T(8,128)S(1)} %add.243), channel_id=1, source_target_pairs={{16,0},{17,1},{18,2},{19,3},{20,4},{21,5},{22,6},{23,7},{24,8},{25... | collective-permute-start | bytes 98312 | tf_op jit(solution)/shard_map/ppermute | solution.py:32
  404.2 33.5 %collective-permute-start.62 = (bf16[128,1024]{1,0:T(8,128)(2,1)}, bf16[128,1024]{1,0:T(8,128)(2,1)S(1)}, u32[]{:S(2)}, u32[]{:S(2)}) collective-permute-start(bf16[128,1024]{1,0:T(8,128)(2,1)} %fusion.1), channel_id=1, source_target_pairs={{8,0},{9,1},{10,2},{11,3},{12,4},{13,5},{14,6},{15,7},{0,8},{1,9},... | collective-permute-start | bytes 786440 | tf_op jit(solution)/shard_map/ppermute | solution.py:32
  431.9 30.8 %collective-permute-start.57 = (bf16[4,3,32,1024]{3,2,1,0:T(8,128)(2,1)S(1)}, bf16[4,3,32,1024]{3,2,1,0:T(8,128)(2,1)S(1)}, u32[]{:S(2)}, u32[]{:S(2)}) collective-permute-start(bf16[4,3,32,1024]{3,2,1,0:T(8,128)(2,1)S(1)} %add_dynamic-update-slice_fusion.6), channel_id=1, source_target_pairs={{2,0},{3,1},{0,2},{1,3},{6,4},{7,5},{4,6},{5,7},{10,8},{11,9},{8,1... | collective-permute-start | bytes 2359304 | tf_op jit(solution)/shard_map/ppermute | solution.py:32
  433.5 29.0 %collective-permute-start.55 = (bf16[2,5,32,1024]{3,2,1,0:T(8,128)(2,1)S(1)}, bf16[2,5,32,1024]{3,2,1,0:T(8,128)(2,1)S(1)}, u32[]{:S(2)}, u32[]{:S(2)}) collective-permute-start(bf16[2,5,32,1024]{3,2,1,0:T(8,128)(2,1)S(1)} %get-tuple-element.419), channel_id=1, source_target_pairs={{16,0},{17,1},{18,2},{19,3},{20,4},{21,5},{22,6},{23,7},{24,8},{25... | collective-permute-start | bytes 1966088 | tf_op jit(solution)/shard_map/ppermute | solution.py:32
  (99 other events, 1431.0 us)
